TPU v7x, 512 devices: a whole 4x8x8 slice. The times are simulated.
512 devices in a mesh: row: 16 (over x, y_hi, core), col: 32 (over y_lo, z).
Axes of the slice: x: 4, y: 8 (y_hi: 2, y_lo: 4; y = y_hi * 4 + y_lo), z: 8, core: 2. Of those that a mesh axis runs over, the one named last changes fastest.
Arguments:
- features: bfloat16 [65536, 512], P(('col', 'row')), may hold values from -6 to 6
- blocks: bfloat16 [16, 32, 48, 128, 128], P('row', 'col'), may hold values from -0.125 to 0.125
- positions: int32 [16, 32, 48], P('row', 'col'), may hold values from 0 to 511, as said below
- counts: int32 [16, 32], P('row', 'col'), may hold values from 8 to 48, as said below
- weight: bfloat16 [512, 512], replicated, may hold values from -0.25 to 0.25
- bias: float32 [512], replicated, may hold values from -3 to 3
- cotangent: bfloat16 [65536, 512], P(('row', 'col')), may hold values from -6 to 6
Outputs:
- activated: bfloat16 [65536, 512], P(('row', 'col'))
- grad_weight: float32 [512, 512], replicated
- grad_bias: float32 [512], replicated
- grad_in: bfloat16 [65536, 512], P(('col', 'row'))
Inputs may be any that keep to these rules, and one draw needn't show every extreme that they name: `counts`: every tile uses between 8 and 24 slots, except exactly one tile, which uses all 48. The 48 positions of one tile are distinct; only the first counts[i, j] of them are used.
All inputs are finite; a program needn't handle non-finite values.
Results may differ from a plain program's by a relative error of at most 0.0069.
Values may be sent and summed in bfloat16 or wider, within the bound.
A program may use at most 64 MiB of HBM per device.

v0:
```python
import jax
import jax.numpy as jnp
from jax import lax
from jax.sharding import Mesh
from jax.sharding import PartitionSpec as P

COL = ("col_0", "col_1")
ROW_COL = ("row", "col_0", "col_1")
COL_ROW = ("col_0", "col_1", "row")


def copy_for_each(x, axis):
    copies = jnp.broadcast_to(x, (lax.axis_size(axis), *x.shape))
    return lax.all_to_all(copies, axis, split_axis=0, concat_axis=0, tiled=True)


def joined_along(tiles, dim):
    shape = list(tiles.shape[1:])
    shape[dim] *= tiles.shape[0]
    return jnp.moveaxis(tiles, 0, dim).reshape(shape)


def gathered_copies(x, axis, dim):
    tiles = copy_for_each(x, axis)
    return joined_along(tiles, dim)


def in_one(arrays, axis):
    vector, at, outs = (jnp.concatenate([a.reshape(-1) for a in arrays]), 0, [])
    total = lax.psum(vector, axis)
    for a in arrays:
        outs.append(total[at : at + a.size].reshape(a.shape))
        at += a.size
    return tuple(outs)


def all_blocks(x, axes, sequence):
    tiles = x
    for k in sequence:
        tiles = lax.all_gather(tiles, axes[k])
    done = sequence[::-1]
    back = [done.index(k) for k in range(len(axes))]
    tiles = tiles.transpose(*back, *range(len(axes), tiles.ndim))
    return tiles.reshape(-1, *x.shape)


def gather_axes(x, axes, sequence, dim):
    return joined_along(all_blocks(x, axes, sequence), dim)


def add_forward(totals, block_vals, slot_pos, start, limit, picked, tile_cols):
    slots = block_vals.shape[0]
    row_index = slot_pos // tile_cols
    products = jnp.einsum("sab,sbf->saf", block_vals, picked, preferred_element_type=jnp.float32)
    alive = (start + jnp.arange(slots, dtype=jnp.int32) < limit).astype(jnp.float32)
    return totals.at[row_index].add(products * alive[:, None, None])


def add_backward(totals, block_vals, slot_pos, start, limit, grad_blocks, tile_cols):
    slots = block_vals.shape[0]
    row_index = slot_pos // tile_cols
    col_index = slot_pos % tile_cols
    picked = jnp.take(grad_blocks, row_index, axis=0)
    products = jnp.einsum("sab,saf->sbf", block_vals, picked, preferred_element_type=jnp.float32)
    alive = (start + jnp.arange(slots, dtype=jnp.int32) < limit).astype(jnp.float32)
    return totals.at[col_index].add(products * alive[:, None, None])


def run_forward(tile_vals, slot_pos, limit, feat_blocks, tile_rows, tile_cols):
    slots = tile_vals.shape[0] // 6
    block = tile_vals.shape[-1]
    width = feat_blocks.shape[-1]

    def one_group(group, totals):
        start = group * slots
        block_vals = lax.dynamic_slice_in_dim(tile_vals, start, slots, 0)
        picked_pos = lax.dynamic_slice_in_dim(slot_pos, start, slots, 0)
        picked = jnp.take(feat_blocks, picked_pos % tile_cols, axis=0)
        return add_forward(totals, block_vals, picked_pos, start, limit, picked, tile_cols)

    return lax.fori_loop(
        0,
        (limit + slots - 1) // slots,
        one_group,
        jnp.zeros((tile_rows, block, width), jnp.float32),
    )


def on_device(features, blocks, positions, counts, weight, bias, cotangent):
    block = blocks.shape[-1]
    width = features.shape[-1]
    col_count = lax.axis_size(COL)
    row_count = lax.axis_size("row")
    gathered = gathered_copies(features, "row", 0)
    tile_cols = gathered.shape[0] // block
    tile_rows = tile_cols * col_count // row_count
    feat_blocks = gathered.reshape(tile_cols, block, width)
    tile_vals = blocks[0, 0]
    slot_pos = positions[0, 0]
    own_count = counts[0, 0]
    slots = tile_vals.shape[0] // 6
    partial_value = run_forward(tile_vals, slot_pos, own_count, feat_blocks, tile_rows, tile_cols)
    share_rows = tile_rows * block // col_count
    sending = partial_value.astype(jnp.bfloat16)
    received = lax.all_to_all(sending, COL, split_axis=0, concat_axis=0, tiled=True)
    summed = jnp.sum(received, axis=0, dtype=jnp.float32)
    aggregated = summed.astype(jnp.bfloat16)
    pre = jnp.dot(aggregated, weight, preferred_element_type=jnp.float32) + bias
    sigma = jax.nn.sigmoid(pre)
    activated = (pre * sigma).astype(jnp.bfloat16)
    grad_pre = (cotangent.astype(jnp.float32) * sigma * (1.0 + pre * (1.0 - sigma))).astype(
        jnp.bfloat16
    )
    weight_term = jnp.einsum("nf,ng->fg", aggregated, grad_pre, preferred_element_type=jnp.float32)
    bias_term = jnp.sum(grad_pre, axis=0, dtype=jnp.float32)
    grad_weight, grad_bias = in_one((weight_term, bias_term), ROW_COL)
    grad_mid = jnp.einsum("ng,fg->nf", grad_pre, weight, preferred_element_type=jnp.float32).astype(
        jnp.bfloat16
    )
    mid_full = gather_axes(grad_mid, COL, (0, 1), 0)
    grad_blocks = mid_full.reshape(tile_rows, block, width)

    def back_group(group, totals):
        start = group * slots
        block_vals = lax.dynamic_slice_in_dim(tile_vals, start, slots, 0)
        picked_pos = lax.dynamic_slice_in_dim(slot_pos, start, slots, 0)
        return add_backward(
            totals, block_vals, picked_pos, start, own_count, grad_blocks, tile_cols
        )

    column_terms = lax.fori_loop(
        0,
        (own_count + slots - 1) // slots,
        back_group,
        jnp.zeros((tile_cols, block, width), jnp.float32),
    )
    back_rows = tile_cols * block // row_count
    back_sending = column_terms.astype(jnp.bfloat16)
    back_received = lax.all_to_all(back_sending, "row", split_axis=0, concat_axis=0, tiled=True)
    grad_in = jnp.sum(back_received, axis=0, dtype=jnp.float32)
    return (activated, grad_weight, grad_bias, grad_in.astype(jnp.bfloat16))


def solution(mesh):
    torus = Mesh(mesh.devices.reshape(mesh.shape["row"], 4, 8), ("row", "col_0", "col_1"))
    return jax.shard_map(
        on_device,
        mesh=torus,
        in_specs=(
            P(COL_ROW, None),
            P("row", COL, None, None, None),
            P("row", COL, None),
            P("row", COL),
            P(),
            P(),
            P(ROW_COL, None),
        ),
        out_specs=(P(ROW_COL, None), P(), P(), P(COL_ROW, None)),
        check_vma=False,
    )
```

profile of v0, /device:TPU:56, one launch (start us, length us, event | category | flops | bytes accessed | tf_op | source)
XLA Modules:
  0.0 663.1 jit_solution(4571801469029452339)
XLA Ops:
  8.0 2.5 broadcast_in_dim.67
  10.5 9.7 %all-to-all-start = ((bf16[16,128,512]{2,1,0:T(8,128)(2,1)}), bf16[16,128,512]{2,1,0:T(8,128)(2,1)}, u32[]{:S(2)}, u32[]{:S(2)}) async-start(bf16[16,128,512]{2,1,0:T(8,128)(2,1)} %broadcast_in_dim.67), calls=%async_computation | async-start | bytes 4194304 | tf_op jit(solution)/shard_map/all_to_all | solution.py:14
  20.9 25.9 %all-to-all-done = bf16[16,128,512]{2,1,0:T(8,128)(2,1)} async-done(((bf16[16,128,512]{2,1,0:T(8,128)(2,1)}), bf16[16,128,512]{2,1,0:T(8,128)(2,1)}, u32[]{:S(2)}, u32[]{:S(2)}) %all-to-all-start) | async-done | bytes 2097184 | tf_op jit(solution)/shard_map/all_to_all | solution.py:14
  46.9 4.3 broadcast_in_dim.66
  51.2 20.2 %while.24 = (s32[]{:T(128)}, f32[32,128,512]{2,1,0:T(8,128)}, s32[]{:T(128)}, s32[48]{0:T(128)S(1)}, bf16[48,128,128]{2,1,0:T(8,128)(2,1)}, /*index=5*/bf16[16,1...) while((s32[]{:T(128)}, f32[32,128,512]{2,1,0:T(8,128)}, ...), condition=%wide.region_2.3_spmd, body=%wide.region_0.2_spmd.sunk | while | flops 135791904 | bytes 11801119 | solution.py:81
  51.9 3.2 gather_fusion
  55.1 1.8 convolution_multiply_fusion.4
  57.0 4.2 scatter_fusion
  61.9 3.2 gather_fusion
  65.1 1.8 convolution_multiply_fusion.4
  67.0 4.4 scatter_fusion
  71.3 4.0 convert_element_type.45
  75.3 140.5 %all_to_all.15 = bf16[32,128,512]{2,1,0:T(8,128)(2,1)} all-to-all(bf16[32,128,512]{2,1,0:T(8,128)(2,1)S(1)} %convert_element_type.45), channel_id=1, replica_groups=mesh['row'=16,'col_0'=4,'col_1'=8] {'col_0','col_1'}, dimensions={0} | all-to-all | bytes 8388608 | tf_op jit(solution)/shard_map/all_to_all | solution.py:105
  215.9 2.8 reduce_sum.33
  220.1 16.8 %all-gather = bf16[512,512]{1,0:T(8,128)(2,1)} all-gather(bf16[128,512]{1,0:T(8,128)(2,1)S(1)} %convolution_convert_fusion), channel_id=2, replica_groups=mesh['row'=16,'col_0'=4,'col_1'=8] {'col_0'}, dimensions={0}, use_global_device_ids=true | all-gather | bytes 655360 | tf_op jit(solution)/shard_map/all_gather | solution.py:40
  236.9 1.6 copy.14
  240.1 53.9 %all-gather.4.cloned.1.call-done = bf16[32,128,512]{2,1,0:T(8,128)(2,1)} async-done(((bf16[4,128,512]{2,1,0:T(8,128)(2,1)}), bf16[32,128,512]{2,1,0:T(8,128)(2,1)}) %all-gather.4.cloned.1.call-update) | async-done | bytes 4194320 | tf_op jit(solution)/shard_map/all_gather | solution.py:40
  293.9 4.6 copy.16
  298.5 2.5 broadcast_in_dim.68
  301.0 21.2 %while.25 = (s32[]{:T(128)}, f32[16,128,512]{2,1,0:T(8,128)}, s32[]{:T(128)}, s32[48]{0:T(128)S(1)}, bf16[48,128,128]{1,2,0:T(8,128)(2,1)}, /*index=5*/bf16[32,1...) while((s32[]{:T(128)}, f32[16,128,512]{2,1,0:T(8,128)}, ...), condition=%wide.region_8.9_spmd, body=%wide.region_6.8_spmd.sunk | while | flops 135791872 | bytes 11801083 | solution.py:131
  301.7 3.8 gather_fusion.1
  305.5 1.8 convolution_multiply_fusion.5
  307.4 4.2 scatter_fusion.1
  312.4 3.8 gather_fusion.1
  316.2 1.8 convolution_multiply_fusion.5
  318.0 4.2 scatter_fusion.1
  322.2 3.8 convert_element_type.51
  326.0 20.1 %all-to-all-start.2 = ((bf16[16,128,512]{2,1,0:T(8,128)(2,1)}), bf16[16,128,512]{2,1,0:T(8,128)(2,1)S(1)}, u32[]{:S(2)}, u32[]{:S(2)}) async-start(bf16[16,128,512]{2,1,0:T(8,128)(2,1)} %convert_element_type.51), calls=%async_computation.2 | async-start | bytes 4194304 | tf_op jit(solution)/shard_map/all_to_all | solution.py:139
  346.1 2.3 pad_maximum_fusion
  348.5 300.3 %all-reduce.2.cloned.1.call-done = f32[262656]{0:T(1024)} async-done(((f32[262656]{0:T(1024)}), f32[262656]{0:T(1024)}) %all-reduce.2.cloned.1.call-update) | async-done | bytes 1050640 | tf_op jit(solution)/shard_map/psum | solution.py:30
  648.8 2.3 slice.23
  651.1 2.4 slice.17
  (33 shorter events, 8.3 us)
Async XLA Ops:
  8.0 210.7 %copy-start = (bf16[512,512]{1,0:T(8,128)(2,1)S(1)}, bf16[512,512]{1,0:T(8,128)(2,1)}, u32[]{:S(2)}) copy-start(bf16[512,512]{1,0:T(8,128)(2,1)} %param.15) | copy-start | bytes 1572868
  10.5 36.3 %all-to-all-start = ((bf16[16,128,512]{2,1,0:T(8,128)(2,1)}), bf16[16,128,512]{2,1,0:T(8,128)(2,1)}, u32[]{:S(2)}, u32[]{:S(2)}) async-start(bf16[16,128,512]{2,1,0:T(8,128)(2,1)} %broadcast_in_dim.67), calls=%async_computation | async-start | bytes 4194304 | tf_op jit(solution)/shard_map/all_to_all | solution.py:14
  20.2 273.7 %all-gather.4.cloned.1.call-start = ((), (), s32[]{:S(2)}) async-start(), calls=%async_computation.4 | async-start | bytes 4718592 | tf_op jit(solution)/shard_map/all_gather | solution.py:40
  46.8 4.3 copy-start.2
  215.9 2.9 copy-start.3
  215.9 2.9 copy-start.4
  218.7 18.1 %copy-start.1 = (bf16[48,128,128]{2,1,0:T(8,128)(2,1)S(1)}, bf16[48,128,128]{2,1,0:T(8,128)(2,1)}, u32[]{:S(2)}) copy-start(bf16[48,128,128]{2,1,0:T(8,128)(2,1)} %get-tuple-element.422) | copy-start | bytes 4718596
  326.0 328.7 %all-to-all-start.2 = ((bf16[16,128,512]{2,1,0:T(8,128)(2,1)}), bf16[16,128,512]{2,1,0:T(8,128)(2,1)S(1)}, u32[]{:S(2)}, u32[]{:S(2)}) async-start(bf16[16,128,512]{2,1,0:T(8,128)(2,1)} %convert_element_type.51), calls=%async_computation.2 | async-start | bytes 4194304 | tf_op jit(solution)/shard_map/all_to_all | solution.py:139
  346.1 302.7 %all-reduce.2.cloned.1.call-start = ((), (), s32[]{:S(2)}) async-start(), calls=%async_computation.3 | async-start | bytes 2105344 | tf_op jit(solution)/shard_map/psum | solution.py:30
Sparse Core Ops, SparseCore 0:
  237.0 56.8 all-gather.3
Sparse Core Ops, SparseCore 1:
  351.6 297.1 all-reduce.1
where the time goes:
time: 665 us; the launch traced here: 663 us
  waiting for transfers between devices  380 us (57%)
  blocking collectives  157 us (24%)
  local copies, waits for them, and re-layouts  36.6 us (6%)
  other arithmetic  34 us (5%)
  starting transfers between devices  29.9 us (4%)
  between operations  16.2 us (2%)
  matrix products  8.83 us (1%)
    psum x1, waiting for transfers between devices, in_one(): total = lax.psum(vector, axis)  300 us
    all_to_all x1, blocking collectives, on_device(): lax.all_to_all(sending, COL, split_axis=0, concat_axis=0, tiled=True)  141 us
    all_gather x1, waiting for transfers between devices, all_blocks(): tiles = lax.all_gather(tiles, axes[k])  53.9 us
    all_to_all x1, waiting for transfers between devices, copy_for_each(): return lax.all_to_all(copies, axis, split_axis=0, concat_axis=0, tiled=True)  25.9 us
    all_to_all x1, starting transfers between devices, on_device(): lax.all_to_all(back_sending, 'row', split_axis=0, concat_axis=0, tiled=True)  20.1 us
    all_gather x1, blocking collectives, all_blocks(): tiles = lax.all_gather(tiles, axes[k])  16.8 us
  transfers between devices with their start and end apart: 4, of which 3 were waited for; matrix products, arithmetic and copies ran while one was open for 2% of the time, Pallas kernels for 0%

commit v1 on v0

v1 whole, which is shorter than its diff:
```python
import jax
import jax.numpy as jnp
from jax import lax
from jax.experimental import pallas as pl
from jax.experimental.pallas import tpu as pltpu
from jax.sharding import Mesh
from jax.sharding import PartitionSpec as P

AXES = ("x", "h", "k", "y", "z")
ROW = ("x", "h", "k")
COL = ("y", "z")
ROW_COL = ROW + COL
COL_ROW = COL + ROW
MESH = pl.DeviceIdType.MESH
NX, NH, NK, NY, NZ = 4, 2, 2, 4, 8
TR, TC = NY * NZ, NX * NH * NK
SLOTS = 48
B = 128
HALF = B // 2
F = 512
FC, FP, FL = 0, SLOTS, 2 * SLOTS
BR, BP, BL = FL + TR, FL + TR + SLOTS, FL + TR + 2 * SLOTS
TABLE = BL + TC
BF16, F32 = jnp.bfloat16, jnp.float32


def link_slots(pos, cnt, tab):
    limit = cnt[0]
    for r in range(TR):
        tab[FL + r] = SLOTS
    for c in range(TC):
        tab[BL + c] = SLOTS

    def one(s, carry):
        p = pos[s]
        r, c = lax.div(p, TC), lax.rem(p, TC)
        live = s < limit
        last_r, last_c = tab[FL + r], tab[BL + c]
        tab[FC + s] = c
        tab[BR + s] = r
        tab[FP + s] = last_r
        tab[BP + s] = last_c
        tab[FL + r] = jnp.where(live, s, last_r)
        tab[BL + c] = jnp.where(live, s, last_c)
        return carry

    lax.fori_loop(0, SLOTS, one, 0)


def layer(
    tab, feat, blocks, weight, bias, cot,
    act_out, gw_out, gb_out, gin_out,
    fall, hist, zs1, zr1, zs, zr, ys, yr, sown, agg, mid, ks, kr, xs1, xr1, xs2, xr2, hs, hr,
    g0, gk, gx, gxr, gz, gzr, gy, gyr, gall,
    send, recv,
):
    x, h, k, y, z = (lax.axis_index(a) for a in AXES)

    def at(name, value):
        return {name: value}

    def xo(d):
        return lax.rem(x + d, NX)

    def zo(d):
        return lax.rem(z + d, NZ)

    def yo(d):
        return lax.rem(y + d, NY)

    hy = h * NY + y

    def y8(d):
        place = lax.rem(hy + d, NH * NY)
        return {"h": lax.div(place, NY), "y": lax.rem(place, NY)}

    other = at("k", 1 - k)
    partner = at("h", 1 - h)

    barrier = pltpu.get_barrier_semaphore()
    greeted = [other]
    greeted += [at("x", xo(d)) for d in range(1, NX)]
    greeted += [at("z", zo(d)) for d in range(1, NZ)]
    greeted += [y8(d) for d in range(1, NH * NY)]
    for device in greeted:
        pl.semaphore_signal(barrier, inc=1, device_id=device, device_id_type=MESH)
    pl.semaphore_wait(barrier, len(greeted))

    used = [0]
    pending = []

    def ids(count):
        first = used[0]
        used[0] += count
        return first

    def copy(src, dst, device, n):
        return pltpu.make_async_remote_copy(
            src_ref=src, dst_ref=dst, send_sem=send.at[n], recv_sem=recv.at[n], device_id=device, device_id_type=MESH
        )

    def go(src, dst, device):
        c = copy(src, dst, device, ids(1))
        c.start()
        pending.append(c)
        return c

    def place(xx, hh, kk):
        return xx * (NH * NK) + hh * NK + kk

    fall[place(x, h, k)] = feat[...]
    lower, upper = pl.ds(0, HALF), pl.ds(HALF, HALF)

    def whole(i, device):
        return go(fall.at[i], fall.at[i], device)

    def part(i, rows, device):
        return go(fall.at[i, rows], fall.at[i, rows], device)

    right, left = at("x", xo(1)), at("x", xo(3))
    own, far = place(x, h, k), place(x, 1 - h, k)
    crossed = []
    to_far = whole(own, partner)
    a_r, a_l = whole(own, right), whole(own, left)
    crossed.append(whole(own, other))
    a_r.wait_recv()
    a_rr = part(place(xo(3), h, k), lower, right)
    crossed.append(whole(place(xo(3), h, k), other))
    a_l.wait_recv()
    a_ll = part(place(xo(1), h, k), upper, left)
    crossed.append(whole(place(xo(1), h, k), other))
    to_far.wait_recv()
    b_r, b_l = whole(far, right), whole(far, left)
    crossed.append(whole(far, other))
    a_rr.wait_recv()
    a_ll.wait_recv()
    crossed.append(whole(place(xo(2), h, k), other))
    b_r.wait_recv()
    b_rr = part(place(xo(3), 1 - h, k), lower, right)
    crossed.append(whole(place(xo(3), 1 - h, k), other))
    b_l.wait_recv()
    b_ll = part(place(xo(1), 1 - h, k), upper, left)
    crossed.append(whole(place(xo(1), 1 - h, k), other))
    b_rr.wait_recv()
    b_ll.wait_recv()
    crossed.append(whole(place(xo(2), 1 - h, k), other))
    for c in crossed:
        c.wait_recv()

    hist[SLOTS] = jnp.zeros((B, F), F32)
    step = 2

    def products(source, index, before, contract):
        def one(g, carry):
            made = []
            for u in range(step):
                s = g * step + u
                made.append(
                    lax.dot_general(
                        blocks[s],
                        source[tab[index + s]],
                        (((contract,), (0,)), ((), ())),
                        preferred_element_type=F32,
                    )
                )
            for u in range(step):
                s = g * step + u
                hist[s] = made[u] + hist[tab[before + s]]
            return carry

        lax.fori_loop(0, SLOTS // step, one, 0)

    products(fall, FC, FP, 1)

    up, down = at("z", zo(1)), at("z", zo(7))
    ways = ((0, up), (1, down))
    z_ids = ids(32)

    def z_copy(n, w, device, t):
        sem = z_ids + n * 8 + w * 4 + t
        if n == 0:
            return copy(zs1.at[w, t], zr1.at[w, t], device, sem)
        return copy(zs.at[w, n - 1, t], zr.at[w, n - 1, t], device, sem)

    def row_sum(r):
        return tab[FL + r]

    for n in range(4):

        def one(t, carry, n=n):
            q = yo(1 + t)
            for w, device in ways:
                slot = row_sum(q * NZ + zo(4 - n if w == 0 else 4 + n))
                if n == 0:
                    zs1[w, t] = hist[slot, w * HALF : (w + 1) * HALF].astype(BF16)
                elif n == 1:
                    z_copy(0, w, device, t).wait_recv()
                    rows, rest = (slice(0, HALF), slice(HALF, B)) if w == 0 else (slice(HALF, B), slice(0, HALF))
                    zs[w, 0, t, rows] = (hist[slot, rows] + zr1[w, t].astype(F32)).astype(BF16)
                    zs[w, 0, t, rest] = hist[slot, rest].astype(BF16)
                else:
                    z_copy(n - 1, w, device, t).wait_recv()
                    zs[w, n - 1, t] = (hist[slot] + zr[w, n - 2, t].astype(F32)).astype(BF16)
                z_copy(n, w, device, t).start()
            return carry

        lax.fori_loop(0, NY, one, 0)

    y_copies = []
    for t in range(NY):
        for w, device in ways:
            z_copy(3, w, device, t).wait_recv()
        total = hist[row_sum(yo(1 + t) * NZ + z)] + zr[0, 2, t].astype(F32) + zr[1, 2, t].astype(F32)
        if t < NY - 1:
            ys[t] = total.astype(BF16)
            y_copies.append(go(ys.at[t], yr.at[t], at("y", yo(1 + t))))
        else:
            sown[...] = total
    for c in y_copies:
        c.wait_recv()
    agg[...] = (
        sown[...] + yr[0].astype(F32) + yr[1].astype(F32) + yr[2].astype(F32)
    ).astype(BF16)

    pre = jnp.dot(agg[...], weight[...], preferred_element_type=F32) + bias[...]
    sigma = jax.nn.sigmoid(pre)
    act_out[...] = (pre * sigma).astype(BF16)
    grad_pre = (cot[...].astype(F32) * sigma * (1.0 + pre * (1.0 - sigma))).astype(BF16)
    mine = y * NZ + z
    mid[mine] = lax.dot_general(
        grad_pre, weight[...], (((1,), (1,)), ((), ())), preferred_element_type=F32
    ).astype(BF16)

    m_ids = ids(32)

    def m_copy(n, w, device, t):
        row = yo(NY - t) * NZ + zo(NZ - n if w == 0 else n)
        sem = m_ids + n * 8 + w * 4 + t
        ref = mid.at[row]
        if n == 3:
            ref = mid.at[row, pl.ds(w * HALF, HALF)]
        return copy(ref, ref, device, sem)

    for w, device in ways:
        m_copy(0, w, device, 0).start()
    y_copies = [go(mid.at[mine], mid.at[mine], at("y", yo(t))) for t in range(1, NY)]
    for t in range(1, NY):
        y_copies[t - 1].wait_recv()
        for w, device in ways:
            m_copy(0, w, device, t).start()

    def forward_step(n):
        def one(t, carry):
            for w, device in ways:
                m_copy(n - 1, w, device, t).wait_recv()
                m_copy(n, w, device, t).start()
            return carry

        lax.fori_loop(0, NY, one, 0)

    gb = jnp.sum(grad_pre.astype(F32), axis=0, keepdims=True)
    bias_rows = jnp.broadcast_to(gb, (8, F))
    for kk in range(NK):
        g0[kk, 0:256] = lax.dot_general(
            agg[:, kk * 256 : (kk + 1) * 256], grad_pre, (((0,), (0,)), ((), ())), preferred_element_type=F32
        )
        g0[kk, 256:264] = bias_rows
    k_copy = go(g0.at[1 - k], gk, other)

    forward_step(1)

    k_copy.wait_recv()
    for xx in range(NX):
        gx[xx, 0:64] = g0[k, xx * 64 : (xx + 1) * 64] + gk[xx * 64 : (xx + 1) * 64]
        gx[xx, 64:72] = g0[k, 256:264] + gk[256:264]
    gxr[x] = gx[x]
    x_copies = [go(gx.at[xo(d)], gxr.at[x], at("x", xo(d))) for d in range(1, NX)]

    forward_step(2)

    for c in x_copies:
        c.wait_recv()
    for zz in range(NZ):
        gz[zz, 0:8] = sum(gxr[i, zz * 8 : (zz + 1) * 8] for i in range(1, NX)) + gxr[0, zz * 8 : (zz + 1) * 8]
        gz[zz, 8:16] = sum(gxr[i, 64:72] for i in range(1, NX)) + gxr[0, 64:72]
    gzr[z] = gz[z]
    zg_copies = [go(gz.at[zo(d)], gzr.at[z], at("z", zo(d))) for d in range(1, NZ)]

    forward_step(3)

    for c in zg_copies:
        c.wait_recv()
    gy[...] = sum(gzr[i] for i in range(1, NZ)) + gzr[0]
    gyr[hy] = gy[...]
    yg_copies = [go(gy, gyr.at[hy], y8(d)) for d in range(1, NH * NY)]

    def last_wait(t, carry):
        for w, device in ways:
            m_copy(3, w, device, t).wait_recv()
        return carry

    lax.fori_loop(0, NY, last_wait, 0)

    for c in yg_copies:
        c.wait_recv()
    g_total = sum(gyr[i] for i in range(1, NH * NY)) + gyr[0]
    gb_out[...] = g_total[8:9]
    gall[k, x, z] = g_total[0:8]
    zg_copies = [go(gall.at[k, x, z], gall.at[k, x, z], at("z", zo(d))) for d in range(1, NZ)]

    products(mid, BR, BP, 0)

    turns = [(1, 2), (0, 2), (1, 1), (1, 3), (0, 1), (0, 3), (1, 0), (0, 0)]

    def hp(dh):
        return 1 - h if dh else h

    k_copies = {}
    for j, (dh, dx) in enumerate(turns):
        ks[j] = hist[tab[BL + place(xo(dx), hp(dh), 1 - k)]].astype(BF16)
        k_copies[j] = go(ks.at[j], kr.at[j], other)

    for c in zg_copies:
        c.wait_recv()
    x_copies = [go(gall.at[k, x], gall.at[k, x], at("x", xo(d))) for d in range(1, NX)]

    first, second, h_copy = {}, {}, None
    for j, (dh, dx) in enumerate(turns):
        k_copies[j].wait_recv()
        slot = tab[BL + place(xo(dx), hp(dh), k)]
        if dx == 2:
            for w, device in ((0, right), (1, left)):
                rows = slice(w * HALF, (w + 1) * HALF)
                xs1[dh, w] = (hist[slot, rows] + kr[j, rows].astype(F32)).astype(BF16)
                first[dh, w] = go(xs1.at[dh, w], xr1.at[dh, w], device)
        elif dx in (1, 3):
            w = 0 if dx == 1 else 1
            first[dh, w].wait_recv()
            rows = slice(w * HALF, (w + 1) * HALF)
            rest = slice((1 - w) * HALF, (2 - w) * HALF)
            xs2[dh, w, rows] = (hist[slot, rows] + kr[j, rows].astype(F32) + xr1[dh, w].astype(F32)).astype(BF16)
            xs2[dh, w, rest] = (hist[slot, rest] + kr[j, rest].astype(F32)).astype(BF16)
            second[dh, w] = go(xs2.at[dh, w], xr2.at[dh, w], right if w == 0 else left)
        else:
            for w in (0, 1):
                second[dh, w].wait_recv()
            total = hist[slot] + kr[j].astype(F32) + xr2[dh, 0].astype(F32) + xr2[dh, 1].astype(F32)
            if dh:
                hs[...] = total.astype(BF16)
                h_copy = go(hs, hr, partner)
            else:
                sown[...] = total

    for c in x_copies:
        c.wait_recv()
    k_copy = go(gall.at[k], gall.at[k], other)

    h_copy.wait_recv()
    gin_out[...] = (sown[...] + hr[...].astype(F32)).astype(BF16)

    k_copy.wait_recv()
    gw_out[...] = gall[...].reshape(F, F)

    def sent(t, carry):
        for n in range(4):
            for w, device in ways:
                z_copy(n, w, device, t).wait_send()
                m_copy(n, w, device, t).wait_send()
        return carry

    lax.fori_loop(0, NY, sent, 0)
    for c in pending:
        c.wait_send()
    assert used[0] <= SEMS


SEMS = 176


def on_device(features, blocks, positions, counts, weight, bias, cotangent):
    smem = pl.BlockSpec(memory_space=pltpu.SMEM)
    vmem = pl.BlockSpec(memory_space=pltpu.VMEM)
    table = pl.pallas_call(
        link_slots,
        out_shape=jax.ShapeDtypeStruct((TABLE,), jnp.int32),
        in_specs=[smem, smem],
        out_specs=smem,
    )(positions.reshape(SLOTS), counts.reshape(1))
    blk = lambda *lead, rows=B, dtype=BF16: pltpu.VMEM((*lead, rows, F), dtype)
    act, gw, gb, gin = pl.pallas_call(
        layer,
        out_shape=[
            jax.ShapeDtypeStruct((B, F), BF16),
            jax.ShapeDtypeStruct((F, F), F32),
            jax.ShapeDtypeStruct((1, F), F32),
            jax.ShapeDtypeStruct((B, F), BF16),
        ],
        in_specs=[smem] + [vmem] * 5,
        out_specs=[vmem] * 4,
        scratch_shapes=[
            blk(TC),
            blk(SLOTS + 1, dtype=F32),
            blk(2, NY, rows=HALF),
            blk(2, NY, rows=HALF),
            blk(2, 3, NY),
            blk(2, 3, NY),
            blk(3),
            blk(3),
            blk(dtype=F32),
            blk(),
            blk(TR),
            blk(8),
            blk(8),
            blk(2, 2, rows=HALF),
            blk(2, 2, rows=HALF),
            blk(2, 2),
            blk(2, 2),
            blk(),
            blk(),
            blk(NK, rows=264, dtype=F32),
            blk(rows=264, dtype=F32),
            blk(NX, rows=72, dtype=F32),
            blk(NX, rows=72, dtype=F32),
            blk(NZ, rows=16, dtype=F32),
            blk(NZ, rows=16, dtype=F32),
            blk(rows=16, dtype=F32),
            blk(NH * NY, rows=16, dtype=F32),
            blk(NK, NX, NZ, rows=8, dtype=F32),
            pltpu.SemaphoreType.DMA((SEMS,)),
            pltpu.SemaphoreType.DMA((SEMS,)),
        ],
        compiler_params=pltpu.CompilerParams(
            collective_id=0, has_side_effects=True, vmem_limit_bytes=56 * 2**20
        ),
    )(table, features, blocks.reshape(SLOTS, B, B), weight, bias.reshape(1, F), cotangent)
    return act, gw, gb.reshape(F), gin


def solution(mesh):
    torus = Mesh(mesh.devices.reshape(NX, NH, NK, NY, NZ), AXES)
    return jax.shard_map(
        on_device,
        mesh=torus,
        in_specs=(
            P(COL_ROW, None),
            P(ROW, COL, None, None, None),
            P(ROW, COL, None),
            P(ROW, COL),
            P(),
            P(),
            P(ROW_COL, None),
        ),
        out_specs=(P(ROW_COL, None), P(), P(), P(COL_ROW, None)),
        check_vma=False,
    )
```

time: 665 us -> 182 us (0.27)
  waiting for transfers between devices: 380 us -> 0 us
  Pallas kernels: 0 us -> 174 us
  blocking collectives: 157 us -> 0 us
  other arithmetic: 34 us -> 0 us
  local copies, waits for them, and re-layouts: 36.6 us -> 5.11 us
  starting transfers between devices: 29.9 us -> 0 us
  between operations: 16.2 us -> 1.31 us
  matrix products: 8.83 us -> 0 us
    psum x1 -> x0, waiting for transfers between devices: 300 us -> none  [in_one(): total = lax.psum(vector, axis)]
    pallas_call x0 -> x2, Pallas kernels: none -> 174 us  [the longest x1 172 us: on_device(): pl.pallas_call(layer, out_shape=[jax.ShapeDtypeStruct((B, F), BF16), jax....]
    all_to_all x1 -> x0, blocking collectives: 141 us -> none  [on_device(): lax.all_to_all(sending, COL, split_axis=0, concat_axis=0, tiled=True)]
    all_gather x1 -> x0, waiting for transfers between devices: 53.9 us -> none  [all_blocks(): tiles = lax.all_gather(tiles, axes[k])]
    all_to_all x2 -> x0, starting transfers between devices: 29.8 us -> none  [the longest x1 20.1 us: on_device(): lax.all_to_all(back_sending, 'row', split_axis=0, concat_axis=0, tiled=True)]
    all_to_all x2 -> x0, waiting for transfers between devices: 25.9 us -> none  [the longest x1 25.9 us: copy_for_each(): return lax.all_to_all(copies, axis, split_axis=0, concat_axis=0, tiled=True)]
    scatter-add x4 -> x0, other arithmetic: 17 us -> none  [the longest x2 8.55 us: add_forward(): return totals.at[row_index].add(products * alive[:, None, None])]
    all_gather x1 -> x0, blocking collectives: 16.8 us -> none  [all_blocks(): tiles = lax.all_gather(tiles, axes[k])]
  transfers between devices with their start and end apart: 4 -> 0, of which waited for: 3 -> 0; matrix products, arithmetic and copies ran while one was open for 2% -> 0% of each run, Pallas kernels for 0% -> 0%
where the time goes in v1:
time: 182 us; the launch traced here: 181 us
  Pallas kernels  174 us (96%)
  local copies, waits for them, and re-layouts  5.11 us (3%)
    pallas_call x1, Pallas kernels, on_device(): pl.pallas_call(layer, out_shape=[jax.ShapeDtypeStruct((B, F), BF16), jax....  172 us
    unnamed x8, local copies, waits for them, and re-layouts  5.11 us

profile of v1, /device:TPU:56, one launch (start us, length us, event | category | flops | bytes accessed | tf_op | source)
XLA Modules:
  0.0 180.5 jit_solution(10111611613834575876)
XLA Ops:
  1.3 2.1 %shard_map.102.tab = s32[240]{0:T(256)} custom-call(s32[48]{0:T(128)} %bitcast.9, s32[1]{0:T(128)} %bitcast.5.cnt), custom_call_target="tpu_custom_call" | custom-call | tf_op jit(solution)/shard_map/pallas_call | solution.py:383
  3.4 172.0 %shard_map.103 = (bf16[128,512]{1,0:T(8,128)(2,1)}, f32[512,512]{1,0:T(8,128)}, f32[1,512]{1,0:T(1,128)}, bf16[128,512]{1,0:T(8,128)(2,1)}) custom-call(s32[240]{0:T(256)} %shard_map.102.tab, bf16[128,512]{1,0:T(8,128)(2,1)} %feat.1, bf16[48,128,128]{2,1,0:T(8,128)(2,1)} %bitcast.6, bf16[512,512]{1,0:T(8,128)(2,1)} %weight.1, f32[1,512]{1,0:T(1,128)} %bitcast.7, ...), custom_call_target="tpu_custom_call" | custom-call | tf_op jit(solution)/shard_map/pallas_call | solution.py:390
  175.4 0.0 copy-start.1
  175.4 0.0 copy-start
  175.4 1.6 copy.16
  177.0 2.3 %copy.17 = f32[512,512]{1,0:T(8,128)} copy(f32[512,512]{1,0:T(8,128)} %get-tuple-element.17) | data formatting | bytes 2097152
  179.3 0.0 copy-done.1
  179.3 0.6 copy.18
  179.9 0.0 copy-done
  179.9 0.7 copy.19
Async XLA Ops:
  175.4 3.9 %copy-start.1 = (f32[1,512]{1,0:T(1,128)S(1)}, f32[1,512]{1,0:T(1,128)}, u32[]{:S(2)}) copy-start(f32[1,512]{1,0:T(1,128)} %get-tuple-element.10) | copy-start | bytes 6148
  175.4 4.5 %copy-start = (bf16[128,512]{1,0:T(8,128)(2,1)S(1)}, bf16[128,512]{1,0:T(8,128)(2,1)}, u32[]{:S(2)}) copy-start(bf16[128,512]{1,0:T(8,128)(2,1)} %get-tuple-element.19) | copy-start | bytes 393220

commit v2 on v1

v2 whole, which is shorter than its diff:
```python
import jax
import jax.numpy as jnp
from jax import lax
from jax.experimental import pallas as pl
from jax.experimental.pallas import tpu as pltpu
from jax.sharding import Mesh
from jax.sharding import PartitionSpec as P

AXES = ("x", "h", "k", "y", "z")
ROW = ("x", "h", "k")
COL = ("y", "z")
ROW_COL = ROW + COL
COL_ROW = COL + ROW
MESH = pl.DeviceIdType.MESH
NX, NH, NK, NY, NZ = 4, 2, 2, 4, 8
TR, TC = NY * NZ, NX * NH * NK
SLOTS = 48
B = 128
HALF = B // 2
F = 512
FC, FP, FL = 0, SLOTS, 2 * SLOTS
BR, BP, BL = FL + TR, FL + TR + SLOTS, FL + TR + 2 * SLOTS
TABLE = BL + TC
BF16, F32 = jnp.bfloat16, jnp.float32


def link_slots(pos, cnt, tab):
    limit = cnt[0]
    for r in range(TR):
        tab[FL + r] = SLOTS
    for c in range(TC):
        tab[BL + c] = SLOTS

    def one(s, carry):
        p = pos[s]
        r, c = lax.div(p, TC), lax.rem(p, TC)
        live = s < limit
        last_r, last_c = tab[FL + r], tab[BL + c]
        tab[FC + s] = c
        tab[BR + s] = r
        tab[FP + s] = last_r
        tab[BP + s] = last_c
        tab[FL + r] = jnp.where(live, s, last_r)
        tab[BL + c] = jnp.where(live, s, last_c)
        return carry

    lax.fori_loop(0, SLOTS, one, 0)


def layer(
    tab, feat, blocks_hbm, weight, bias, cot,
    act_out, gw_out, gb_out, gin_out,
    blocks, fall_0, fall_1, hist, zs1, zr1, zs, zr, ys, yr, own_sum, agg, mid_0, mid_1, ks, kr, xs, xr, hs, hr,
    g0, gk, gx, gxr, gy, gyr, gz, gzr, gall,
    send, recv, fetched,
):
    x, h, k, y, z = (lax.axis_index(a) for a in AXES)
    fall, mid = (fall_0, fall_1), (mid_0, mid_1)
    fetch = pltpu.make_async_copy(blocks_hbm, blocks, fetched)
    fetch.start()

    def at(name, value):
        return {name: value}

    def xo(d):
        return lax.rem(x + d, NX)

    def zo(d):
        return lax.rem(z + d, NZ)

    def yo(d):
        return lax.rem(y + d, NY)

    hy = h * NY + y

    def y8(d):
        place = lax.rem(hy + d, NH * NY)
        return {"h": lax.div(place, NY), "y": lax.rem(place, NY)}

    other = at("k", 1 - k)
    partner = at("h", 1 - h)
    up, down = at("z", zo(1)), at("z", zo(7))
    ways = ((0, up), (1, down))
    chunks = range(CHUNKS)
    cols = [slice(c * W, (c + 1) * W) for c in chunks]

    barrier = pltpu.get_barrier_semaphore()
    greeted = [other]
    greeted += [at("x", xo(d)) for d in range(1, NX)]
    greeted += [at("z", zo(d)) for d in range(1, NZ)]
    greeted += [y8(d) for d in range(1, NH * NY)]
    for device in greeted:
        pl.semaphore_signal(barrier, inc=1, device_id=device, device_id_type=MESH)

    def place(xx, hh, kk):
        return xx * (NH * NK) + hh * NK + kk

    own, far = place(x, h, k), place(x, 1 - h, k)
    for c in chunks:
        fall[c][own] = feat[:, cols[c]]
        hist[c, SLOTS] = jnp.zeros((B, W), F32)
    pl.semaphore_wait(barrier, len(greeted))

    used = [0]
    pending = []

    def ids(count):
        first = used[0]
        used[0] += count
        return first

    def copy(src, dst, device, n):
        return pltpu.make_async_remote_copy(
            src_ref=src, dst_ref=dst, send_sem=send.at[n], recv_sem=recv.at[n], device_id=device, device_id_type=MESH
        )

    def go(src, dst, device):
        c = copy(src, dst, device, ids(1))
        c.start()
        pending.append(c)
        return c

    def received(copies):
        for c in copies:
            c.wait_recv()

    def features(c):
        def whole(i, device):
            return go(fall[c].at[i], fall[c].at[i], device)

        to_far = whole(own, partner)
        own_x = [whole(own, at("x", xo(d))) for d in TURNS]
        crossed = [whole(own, other)]
        yield
        to_far.wait_recv()
        far_x = [whole(far, at("x", xo(d))) for d in TURNS]
        crossed.append(whole(far, other))
        yield
        for d, c_x in zip(TURNS, own_x):
            c_x.wait_recv()
            crossed.append(whole(place(xo(NX - d), h, k), other))
        yield
        for d, c_x in zip(TURNS, far_x):
            c_x.wait_recv()
            crossed.append(whole(place(xo(NX - d), 1 - h, k), other))
        yield
        received(crossed)
        yield

    step = 8

    def products(c, source, index, before, contract):
        def one(g, carry):
            made = []
            for u in range(step):
                s = g * step + u
                made.append(
                    lax.dot_general(
                        blocks[s],
                        source[c][tab[index + s]],
                        (((contract,), (0,)), ((), ())),
                        preferred_element_type=F32,
                    )
                )
            for u in range(step):
                s = g * step + u
                hist[c, s] = made[u] + hist[c, tab[before + s]]
            return carry

        lax.fori_loop(0, SLOTS // step, one, 0)

    z_ids = ids(32 * CHUNKS)

    def z_copy(n, c, w, device, t):
        sem = z_ids + ((c * 4 + n) * 2 + w) * NY + t
        if n == 0:
            return copy(zs1.at[c, w, t], zr1.at[c, w, t], device, sem)
        return copy(zs.at[c, w, n - 1, t], zr.at[c, w, n - 1, t], device, sem)

    def scatter_step(n, c):
        def one(t, carry):
            q = yo(1 + t)
            for w, device in ways:
                slot = tab[FL + q * NZ + zo(4 - n if w == 0 else 4 + n)]
                if n == 0:
                    zs1[c, w, t] = hist[c, slot, w * HALF : (w + 1) * HALF].astype(BF16)
                elif n == 1:
                    z_copy(0, c, w, device, t).wait_recv()
                    rows, rest = (slice(0, HALF), slice(HALF, B)) if w == 0 else (slice(HALF, B), slice(0, HALF))
                    zs[c, w, 0, t, rows] = (hist[c, slot, rows] + zr1[c, w, t].astype(F32)).astype(BF16)
                    zs[c, w, 0, t, rest] = hist[c, slot, rest].astype(BF16)
                else:
                    z_copy(n - 1, c, w, device, t).wait_recv()
                    zs[c, w, n - 1, t] = (hist[c, slot] + zr[c, w, n - 2, t].astype(F32)).astype(BF16)
                z_copy(n, c, w, device, t).start()
            return carry

        lax.fori_loop(0, NY, one, 0)

    y_copies = []

    def scatter_y(c):
        for t in range(NY):
            for w, device in ways:
                z_copy(3, c, w, device, t).wait_recv()
            slot = tab[FL + yo(1 + t) * NZ + z]
            total = hist[c, slot] + zr[c, 0, 2, t].astype(F32) + zr[c, 1, 2, t].astype(F32)
            if t < NY - 1:
                ys[c, t] = total.astype(BF16)
                y_copies.append(go(ys.at[c, t], yr.at[c, t], at("y", yo(1 + t))))
            else:
                own_sum[c] = total

    first, later = (features(c) for c in chunks)
    next(first)
    next(first)
    next(later)
    next(first)
    next(first)
    next(first)
    fetch.wait()
    products(0, fall, FC, FP, 1)
    scatter_step(0, 0)
    next(later)
    scatter_step(1, 0)
    next(later)
    next(later)
    scatter_step(2, 0)
    next(later)
    products(1, fall, FC, FP, 1)
    scatter_step(0, 1)
    scatter_step(3, 0)
    scatter_step(1, 1)
    scatter_y(0)
    scatter_step(2, 1)
    scatter_step(3, 1)
    scatter_y(1)
    received(y_copies)
    for c in chunks:
        agg[:, cols[c]] = (
            own_sum[c] + yr[c, 0].astype(F32) + yr[c, 1].astype(F32) + yr[c, 2].astype(F32)
        ).astype(BF16)

    pre = jnp.dot(agg[...], weight[...], preferred_element_type=F32) + bias[...]
    sigma = jax.nn.sigmoid(pre)
    act_out[...] = (pre * sigma).astype(BF16)
    grad_pre = (cot[...].astype(F32) * sigma * (1.0 + pre * (1.0 - sigma))).astype(BF16)
    mine = y * NZ + z
    m_ids = ids(32 * CHUNKS)

    def m_copy(n, c, w, device, t):
        row = yo(NY - t) * NZ + zo(NZ - n if w == 0 else n)
        sem = m_ids + ((c * 4 + n) * 2 + w) * NY + t
        ref = mid[c].at[row]
        if n == 3:
            ref = mid[c].at[row, pl.ds(w * HALF, HALF)]
        return copy(ref, ref, device, sem)

    m_y = []
    for c in chunks:
        mid[c][mine] = lax.dot_general(
            grad_pre, weight[cols[c], :], (((1,), (1,)), ((), ())), preferred_element_type=F32
        ).astype(BF16)
        if c == 0:
            for w, device in ways:
                m_copy(0, c, w, device, 0).start()
        m_y.append([go(mid[c].at[mine], mid[c].at[mine], at("y", yo(t))) for t in range(1, NY)])

    def gather_first(c):
        if c > 0:
            for w, device in ways:
                m_copy(0, c, w, device, 0).start()
        for t in range(1, NY):
            m_y[c][t - 1].wait_recv()
            for w, device in ways:
                m_copy(0, c, w, device, t).start()

    def gather_step(n, c):
        def one(t, carry):
            for w, device in ways:
                m_copy(n - 1, c, w, device, t).wait_recv()
                m_copy(n, c, w, device, t).start()
            return carry

        lax.fori_loop(0, NY, one, 0)

    def gather_last(c):
        def one(t, carry):
            for w, device in ways:
                m_copy(3, c, w, device, t).wait_recv()
            return carry

        lax.fori_loop(0, NY, one, 0)

    def gradients():
        gb = jnp.sum(grad_pre.astype(F32), axis=0, keepdims=True)
        bias_rows = jnp.broadcast_to(gb, (8, F))
        for kk in range(NK):
            g0[kk, 0:256] = lax.dot_general(
                agg[:, kk * 256 : (kk + 1) * 256], grad_pre, (((0,), (0,)), ((), ())), preferred_element_type=F32
            )
            g0[kk, 256:264] = bias_rows
        k_copy = go(g0.at[1 - k], gk, other)
        yield
        k_copy.wait_recv()
        for i in range(NX):
            gx[i, 0:64] = g0[k, i * 64 : (i + 1) * 64] + gk[i * 64 : (i + 1) * 64]
            gx[i, 64:72] = g0[k, 256:264] + gk[256:264]
        gxr[x] = gx[x]
        copies = [go(gx.at[xo(d)], gxr.at[x], at("x", xo(d))) for d in range(1, NX)]
        yield
        received(copies)
        bias_sum = gxr[0, 64:72] + gxr[1, 64:72] + gxr[2, 64:72] + gxr[3, 64:72]
        for i in range(NH * NY):
            rows = slice(i * 8, (i + 1) * 8)
            gy[i, 0:8] = gxr[0, rows] + gxr[1, rows] + gxr[2, rows] + gxr[3, rows]
            gy[i, 8:16] = bias_sum
        gyr[hy] = gy[hy]
        copies = [go(gy.at[lax.rem(hy + d, NH * NY)], gyr.at[hy], y8(d)) for d in range(1, NH * NY)]
        yield
        received(copies)
        total = gyr[0]
        for i in range(1, NH * NY):
            total += gyr[i]
        gz[...] = total.astype(BF16)
        gzr[z] = gz[...]
        copies = [go(gz, gzr.at[z], at("z", zo(d))) for d in range(1, NZ)]
        yield
        received(copies)
        total = gzr[0].astype(F32)
        for i in range(1, NZ):
            total += gzr[i].astype(F32)
        gb_out[...] = total[8:9]
        gall[k, x, hy] = total[0:8]
        copies = [go(gall.at[k, x, hy], gall.at[k, x, hy], y8(d)) for d in range(1, NH * NY)]
        yield
        received(copies)
        copies = [go(gall.at[k, x], gall.at[k, x], at("x", xo(d))) for d in range(1, NX)]
        yield
        received(copies)
        k_copy = go(gall.at[k], gall.at[k], other)
        yield
        k_copy.wait_recv()
        gw_out[...] = gall[...].reshape(F, F)
        yield

    def hp(dh):
        return 1 - h if dh else h

    turns = [(dh, dx) for dh in (1, 0) for dx in (*TURNS, 0)]

    def back(c):
        k_copies = []
        for j, (dh, dx) in enumerate(turns):
            ks[c, j] = hist[c, tab[BL + place(xo(dx), hp(dh), 1 - k)]].astype(BF16)
            k_copies.append(go(ks.at[c, j], kr.at[c, j], other))
        yield

        def term(j):
            dh, dx = turns[j]
            return hist[c, tab[BL + place(xo(dx), hp(dh), k)]] + kr[c, j].astype(F32)

        x_copies = {0: [], 1: []}
        for j, (dh, dx) in enumerate(turns):
            k_copies[j].wait_recv()
            if dx:
                xs[c, dh, dx - 1] = term(j).astype(BF16)
                x_copies[dh].append(go(xs.at[c, dh, dx - 1], xr.at[c, dh, dx - 1], at("x", xo(dx))))
        yield
        for dh in (1, 0):
            received(x_copies[dh])
            total = term(turns.index((dh, 0)))
            for i in range(NX - 1):
                total += xr[c, dh, i].astype(F32)
            if dh:
                hs[c] = total.astype(BF16)
                h_copy = go(hs.at[c], hr.at[c], partner)
            else:
                own_sum[c] = total
        yield
        h_copy.wait_recv()
        gin_out[:, cols[c]] = (own_sum[c] + hr[c].astype(F32)).astype(BF16)
        yield

    grads = gradients()
    backs = [back(c) for c in chunks]
    gather_first(0)
    next(grads)
    gather_step(1, 0)
    next(grads)
    gather_step(2, 0)
    gather_first(1)
    gather_step(3, 0)
    next(grads)
    gather_step(1, 1)
    gather_last(0)
    products(0, mid, BR, BP, 0)
    next(backs[0])
    gather_step(2, 1)
    next(backs[0])
    next(grads)
    gather_step(3, 1)
    next(backs[0])
    next(grads)
    gather_last(1)
    products(1, mid, BR, BP, 0)
    next(backs[1])
    next(backs[0])
    next(grads)
    next(backs[1])
    next(grads)
    next(backs[1])
    next(backs[1])
    next(grads)

    def sent(t, carry):
        for c in chunks:
            for n in range(4):
                for w, device in ways:
                    z_copy(n, c, w, device, t).wait_send()
                    m_copy(n, c, w, device, t).wait_send()
        return carry

    lax.fori_loop(0, NY, sent, 0)
    for c in pending:
        c.wait_send()
    assert used[0] <= SEMS


CHUNKS = 2
TURNS = (1, 3, 2)
W = F // CHUNKS
SEMS = 256


def hand_over(*refs):
    for source, target in zip(refs[: len(refs) // 2], refs[len(refs) // 2 :]):
        target[...] = source[...]


def on_device(features, blocks, positions, counts, weight, bias, cotangent):
    smem = pl.BlockSpec(memory_space=pltpu.SMEM)
    vmem = pl.BlockSpec(memory_space=pltpu.VMEM)
    table = pl.pallas_call(
        link_slots,
        out_shape=jax.ShapeDtypeStruct((TABLE,), jnp.int32),
        in_specs=[smem, smem],
        out_specs=smem,
    )(positions.reshape(SLOTS), counts.reshape(1))

    def chunk(*lead, rows=B, dtype=BF16):
        return pltpu.VMEM((CHUNKS, *lead, rows, W), dtype)

    def part(*lead):
        return pltpu.VMEM((*lead, B, W), BF16)

    def full(*lead, rows, dtype=F32):
        return pltpu.VMEM((*lead, rows, F), dtype)

    outs = [
        jax.ShapeDtypeStruct((B, F), BF16),
        jax.ShapeDtypeStruct((F, F), F32),
        jax.ShapeDtypeStruct((1, F), F32),
        jax.ShapeDtypeStruct((B, F), BF16),
    ]
    results = pl.pallas_call(
        layer,
        out_shape=outs,
        in_specs=[smem, vmem, pl.BlockSpec(memory_space=pl.ANY), vmem, vmem, vmem],
        out_specs=[vmem] * 4,
        scratch_shapes=[
            pltpu.VMEM((SLOTS, B, B), BF16),
            part(TC),
            part(TC),
            chunk(SLOTS + 1, dtype=F32),
            chunk(2, NY, rows=HALF),
            chunk(2, NY, rows=HALF),
            chunk(2, 3, NY),
            chunk(2, 3, NY),
            chunk(3),
            chunk(3),
            chunk(dtype=F32),
            full(rows=B, dtype=BF16),
            part(TR),
            part(TR),
            chunk(8),
            chunk(8),
            chunk(2, 3),
            chunk(2, 3),
            chunk(),
            chunk(),
            full(NK, rows=264),
            full(rows=264),
            full(NX, rows=72),
            full(NX, rows=72),
            full(NH * NY, rows=16),
            full(NH * NY, rows=16),
            full(rows=16, dtype=BF16),
            full(NZ, rows=16, dtype=BF16),
            full(NK, NX, NH * NY, rows=8),
            pltpu.SemaphoreType.DMA((SEMS,)),
            pltpu.SemaphoreType.DMA((SEMS,)),
            pltpu.SemaphoreType.DMA,
        ],
        compiler_params=pltpu.CompilerParams(
            collective_id=0, has_side_effects=True, vmem_limit_bytes=56 * 2**20
        ),
    )(table, features, blocks.reshape(SLOTS, B, B), weight, bias.reshape(1, F), cotangent)
    act, gw, gb, gin = pl.pallas_call(hand_over, out_shape=outs, in_specs=[vmem] * 4, out_specs=[vmem] * 4)(*results)
    return act, gw, gb.reshape(F), gin


def solution(mesh):
    torus = Mesh(mesh.devices.reshape(NX, NH, NK, NY, NZ), AXES)
    return jax.shard_map(
        on_device,
        mesh=torus,
        in_specs=(
            P(COL_ROW, None),
            P(ROW, COL, None, None, None),
            P(ROW, COL, None),
            P(ROW, COL),
            P(),
            P(),
            P(ROW_COL, None),
        ),
        out_specs=(P(ROW_COL, None), P(), P(), P(COL_ROW, None)),
        check_vma=False,
    )
```

time: 182 us -> 157 us (0.86)
  Pallas kernels: 174 us -> 155 us
  local copies, waits for them, and re-layouts: 5.11 us -> 0 us
    pallas_call x1 -> x2, Pallas kernels: 172 us -> 153 us  [the longest x1 151 us: on_device(): pl.pallas_call(layer, out_shape=outs, in_specs=[smem, vmem, pl.BlockSpec(...]
    unnamed x8 -> x0, local copies, waits for them, and re-layouts: 5.11 us -> none
where the time goes in v2:
time: 157 us
  Pallas kernels  155 us (99%)
    pallas_call x1, Pallas kernels, on_device(): pl.pallas_call(layer, out_shape=outs, in_specs=[smem, vmem, pl.BlockSpec(...  151 us

profile of v2, /device:TPU:56, one launch (start us, length us, event | category | flops | bytes accessed | tf_op | source)
XLA Modules:
  0.0 156.7 jit_solution(8992218359246329615)
XLA Ops:
  1.3 2.1 %shard_map.102.tab = s32[240]{0:T(256)} custom-call(s32[48]{0:T(128)} %bitcast.8, s32[1]{0:T(128)} %bitcast.5.cnt), custom_call_target="tpu_custom_call" | custom-call | tf_op jit(solution)/shard_map/pallas_call | solution.py:444
  3.4 151.0 %shard_map.103 = (bf16[128,512]{1,0:T(8,128)(2,1)}, f32[512,512]{1,0:T(8,128)}, f32[1,512]{1,0:T(1,128)}, bf16[128,512]{1,0:T(8,128)(2,1)}) custom-call(s32[240]{0:T(256)} %shard_map.102.tab, bf16[128,512]{1,0:T(8,128)(2,1)} %feat.1, bf16[48,128,128]{2,1,0:T(8,128)(2,1)} %bitcast.6, bf16[512,512]{1,0:T(8,128)(2,1)} %weight.1, f32[1,512]{1,0:T(1,128)} %bitcast.7, ...), custom_call_target="tpu_custom_call" | custom-call | tf_op jit(solution)/shard_map/pallas_call | solution.py:466
  154.4 2.4 %shard_map.104 = (bf16[128,512]{1,0:T(8,128)(2,1)}, f32[512,512]{1,0:T(8,128)}, f32[1,512]{1,0:T(1,128)}, bf16[128,512]{1,0:T(8,128)(2,1)}) custom-call(bf16[128,512]{1,0:T(8,128)(2,1)} %get-tuple-element.12.refs_0_, f32[512,512]{1,0:T(8,128)} %get-tuple-element.13.refs_1_, f32[1,512]{1,0:T(1,128)} %get-tuple-element.14.refs_2_, ...), custom_call_target="tpu_custom_call" | custom-call | tf_op jit(solution)/shard_map/pallas_call | solution.py:509

commit v3 on v2

--- a/solution.py
+++ b/solution.py
@@ -48,16 +48,34 @@
 
 
 def layer(
-    tab, feat, blocks_hbm, weight, bias, cot,
-    act_out, gw_out, gb_out, gin_out,
-    blocks, fall_0, fall_1, hist, zs1, zr1, zs, zr, ys, yr, own_sum, agg, mid_0, mid_1, ks, kr, xs, xr, hs, hr,
+    tab_hbm, feat_hbm, blocks_hbm, weight_hbm, bias_hbm, cot_hbm,
+    act_hbm, gw_hbm, gb_hbm, gin_hbm,
+    tab, weight, bias, cot, act_out, gb_out, gin_out, blocks, fall_0, fall_1, hist, zs1, zr1, zs, zr, ys, yr, oz, y1s, y1r, y2s1, y2r1, y2s, y2r, own_sum, agg, mid_0, mid_1, mid_y, ks, kr, xs, xr, hs, hr,
     g0, gk, gx, gxr, gy, gyr, gz, gzr, gall,
-    send, recv, fetched,
+    send, recv, local,
 ):
     x, h, k, y, z = (lax.axis_index(a) for a in AXES)
     fall, mid = (fall_0, fall_1), (mid_0, mid_1)
-    fetch = pltpu.make_async_copy(blocks_hbm, blocks, fetched)
-    fetch.start()
+    narrow, early, wide = slice(0, V), slice(V, 2 * V), slice(2 * V, F)
+    z_cols, z_hist = (narrow, wide), (slice(0, V), slice(0, W))
+    own = (lax.axis_index("x") * NH + lax.axis_index("h")) * NK + lax.axis_index("k")
+    f_in = [pltpu.make_async_copy(feat_hbm.at[:, pl.ds(c * W, W)], fall[c].at[own], local.at[c]) for c in range(CHUNKS)]
+    early_in = [pltpu.make_async_copy(tab_hbm, tab, local.at[2]), pltpu.make_async_copy(blocks_hbm, blocks, local.at[3])]
+    late_in = [
+        pltpu.make_async_copy(weight_hbm, weight, local.at[4]),
+        pltpu.make_async_copy(bias_hbm, bias, local.at[5]),
+        pltpu.make_async_copy(cot_hbm, cot, local.at[6]),
+    ]
+    for c in (*f_in, *early_in, *late_in):
+        c.start()
+    act_store = pltpu.make_async_copy(act_out, act_hbm, local.at[7])
+    gb_store = pltpu.make_async_copy(gb_out, gb_hbm, local.at[8])
+    gin_store = pltpu.make_async_copy(gin_out, gin_hbm, local.at[9])
+    stores = []
+
+    def store(c):
+        c.start()
+        stores.append(c)
 
     def at(name, value):
         return {name: value}
@@ -95,10 +113,11 @@
     def place(xx, hh, kk):
         return xx * (NH * NK) + hh * NK + kk
 
-    own, far = place(x, h, k), place(x, 1 - h, k)
+    far = place(x, 1 - h, k)
     for c in chunks:
-        fall[c][own] = feat[:, cols[c]]
         hist[c, SLOTS] = jnp.zeros((B, W), F32)
+    for c in f_in:
+        c.wait()
     pl.semaphore_wait(barrier, len(greeted))
 
     used = [0]
@@ -157,7 +176,7 @@
                 made.append(
                     lax.dot_general(
                         blocks[s],
-                        source[c][tab[index + s]],
+                        source(tab[index + s]),
                         (((contract,), (0,)), ((), ())),
                         preferred_element_type=F32,
                     )
@@ -174,24 +193,28 @@
     def z_copy(n, c, w, device, t):
         sem = z_ids + ((c * 4 + n) * 2 + w) * NY + t
         if n == 0:
-            return copy(zs1.at[c, w, t], zr1.at[c, w, t], device, sem)
-        return copy(zs.at[c, w, n - 1, t], zr.at[c, w, n - 1, t], device, sem)
+            return copy(zs1[c].at[w, t], zr1[c].at[w, t], device, sem)
+        return copy(zs[c].at[w, n - 1, t], zr[c].at[w, n - 1, t], device, sem)
+
+    def term(c, row, rows=slice(0, B)):
+        return hist[c, tab[FL + row], rows, z_hist[c]]
+
+    halves = (slice(0, HALF), slice(HALF, B))
 
     def scatter_step(n, c):
         def one(t, carry):
             q = yo(1 + t)
             for w, device in ways:
-                slot = tab[FL + q * NZ + zo(4 - n if w == 0 else 4 + n)]
+                row = q * NZ + zo(4 - n if w == 0 else 4 + n)
                 if n == 0:
-                    zs1[c, w, t] = hist[c, slot, w * HALF : (w + 1) * HALF].astype(BF16)
+                    zs1[c][w, t] = term(c, row, halves[w]).astype(BF16)
                 elif n == 1:
                     z_copy(0, c, w, device, t).wait_recv()
-                    rows, rest = (slice(0, HALF), slice(HALF, B)) if w == 0 else (slice(HALF, B), slice(0, HALF))
-                    zs[c, w, 0, t, rows] = (hist[c, slot, rows] + zr1[c, w, t].astype(F32)).astype(BF16)
-                    zs[c, w, 0, t, rest] = hist[c, slot, rest].astype(BF16)
+                    zs[c][w, 0, t, halves[w]] = (term(c, row, halves[w]) + zr1[c][w, t].astype(F32)).astype(BF16)
+                    zs[c][w, 0, t, halves[1 - w]] = term(c, row, halves[1 - w]).astype(BF16)
                 else:
                     z_copy(n - 1, c, w, device, t).wait_recv()
-                    zs[c, w, n - 1, t] = (hist[c, slot] + zr[c, w, n - 2, t].astype(F32)).astype(BF16)
+                    zs[c][w, n - 1, t] = (term(c, row) + zr[c][w, n - 2, t].astype(F32)).astype(BF16)
                 z_copy(n, c, w, device, t).start()
             return carry
 
@@ -203,13 +226,54 @@
         for t in range(NY):
             for w, device in ways:
                 z_copy(3, c, w, device, t).wait_recv()
-            slot = tab[FL + yo(1 + t) * NZ + z]
-            total = hist[c, slot] + zr[c, 0, 2, t].astype(F32) + zr[c, 1, 2, t].astype(F32)
+            total = term(c, yo(1 + t) * NZ + z) + zr[c][0, 2, t].astype(F32) + zr[c][1, 2, t].astype(F32)
             if t < NY - 1:
-                ys[c, t] = total.astype(BF16)
-                y_copies.append(go(ys.at[c, t], yr.at[c, t], at("y", yo(1 + t))))
+                ys[c][t] = total.astype(BF16)
+                y_copies.append(go(ys[c].at[t], yr[c].at[t], at("y", yo(1 + t))))
             else:
-                own_sum[c] = total
+                oz[c][...] = total
+
+    order = (4, 3, 5, 2, 6, 1, 7, 0)
+    groups = (slice(0, 1), slice(1, 3), slice(3, 5), slice(5, 7), slice(7, 8))
+    early_hist = slice(V, 2 * V)
+    early_y, early_z = [], {}
+
+    def early_send():
+        for group in groups:
+            copies = []
+            for d in range(1, NY):
+                for p in range(group.start, group.stop):
+                    y1s[d - 1, p] = hist[0, tab[FL + yo(d) * NZ + zo(order[p])], :, early_hist].astype(BF16)
+                part = pl.ds(group.start, group.stop - group.start)
+                copies.append(go(y1s.at[d - 1, part], y1r.at[d - 1, part], at("y", yo(d))))
+            early_y.append(copies)
+
+    def early_term(p, rows=slice(0, B)):
+        total = hist[0, tab[FL + y * NZ + zo(order[p])], rows, early_hist]
+        for d in range(NY - 1):
+            total += y1r[d, p, rows].astype(F32)
+        return total
+
+    def early_step(n):
+        received(early_y[n])
+        for w, device in ways:
+            if n == 0:
+                y2s1[w] = early_term(0, halves[w]).astype(BF16)
+                early_z[0, w] = go(y2s1.at[w], y2r1.at[w], device)
+                continue
+            early_z[n - 1, w].wait_recv()
+            p = 2 * n - 1 + w
+            if n == 1:
+                y2s[w, 0, halves[w]] = (early_term(p, halves[w]) + y2r1[w].astype(F32)).astype(BF16)
+                y2s[w, 0, halves[1 - w]] = early_term(p, halves[1 - w]).astype(BF16)
+            else:
+                y2s[w, n - 1] = (early_term(p) + y2r[w, n - 2].astype(F32)).astype(BF16)
+            early_z[n, w] = go(y2s.at[w, n - 1], y2r.at[w, n - 1], device)
+
+    def early_last():
+        received(early_y[4])
+        received([early_z[3, 0], early_z[3, 1]])
+        agg[:, early] = (early_term(7) + y2r[0, 2].astype(F32) + y2r[1, 2].astype(F32)).astype(BF16)
 
     first, later = (features(c) for c in chunks)
     next(first)
@@ -218,32 +282,42 @@
     next(first)
     next(first)
     next(first)
-    fetch.wait()
-    products(0, fall, FC, FP, 1)
+    for c in early_in:
+        c.wait()
+    products(0, lambda i: fall[0][i], FC, FP, 1)
     scatter_step(0, 0)
+    early_send()
     next(later)
     scatter_step(1, 0)
     next(later)
     next(later)
+    early_step(0)
     scatter_step(2, 0)
     next(later)
-    products(1, fall, FC, FP, 1)
+    products(1, lambda i: fall[1][i], FC, FP, 1)
     scatter_step(0, 1)
     scatter_step(3, 0)
+    early_step(1)
     scatter_step(1, 1)
+    early_step(2)
     scatter_y(0)
     scatter_step(2, 1)
+    early_step(3)
     scatter_step(3, 1)
+    early_last()
     scatter_y(1)
     received(y_copies)
     for c in chunks:
-        agg[:, cols[c]] = (
-            own_sum[c] + yr[c, 0].astype(F32) + yr[c, 1].astype(F32) + yr[c, 2].astype(F32)
+        agg[:, z_cols[c]] = (
+            oz[c][...] + yr[c][0].astype(F32) + yr[c][1].astype(F32) + yr[c][2].astype(F32)
         ).astype(BF16)
 
+    for c in late_in:
+        c.wait()
     pre = jnp.dot(agg[...], weight[...], preferred_element_type=F32) + bias[...]
     sigma = jax.nn.sigmoid(pre)
     act_out[...] = (pre * sigma).astype(BF16)
+    store(act_store)
     grad_pre = (cot[...].astype(F32) * sigma * (1.0 + pre * (1.0 - sigma))).astype(BF16)
     mine = y * NZ + z
     m_ids = ids(32 * CHUNKS)
@@ -256,18 +330,52 @@
             ref = mid[c].at[row, pl.ds(w * HALF, HALF)]
         return copy(ref, ref, device, sem)
 
-    m_y = []
-    for c in chunks:
-        mid[c][mine] = lax.dot_general(
-            grad_pre, weight[cols[c], :], (((1,), (1,)), ((), ())), preferred_element_type=F32
+    def grad_mid(part):
+        return lax.dot_general(
+            grad_pre, weight[part, :], (((1,), (1,)), ((), ())), preferred_element_type=F32
         ).astype(BF16)
-        if c == 0:
+
+    m_y = {}
+    e_ids = ids(8)
+    e_y = []
+
+    def e_copy(n, w, device):
+        row = y * NZ + zo(NZ - n if w == 0 else n)
+        ref = mid_y.at[row]
+        if n == 3:
+            ref = mid_y.at[row, pl.ds(w * HALF, HALF)]
+        return copy(ref, ref, device, e_ids + n * 2 + w)
+
+    def e_spread(row):
+        for t in range(1, NY):
+            e_y.append(go(mid_y.at[row], mid_y.at[row], at("y", yo(t))))
+
+    def early_gather(n):
+        for w, device in ways:
+            if n > 0:
+                e_copy(n - 1, w, device).wait_recv()
+            if n < 4:
+                e_copy(n, w, device).start()
+        if n == 0:
+            e_spread(mine)
+        elif n < 4:
+            e_spread(y * NZ + zo(NZ - n))
+            e_spread(y * NZ + zo(n))
+        else:
+            e_spread(y * NZ + zo(4))
+
+    for c in (1, 0):
+        mid[c][mine] = grad_mid(z_cols[c])
+        if c == 1:
             for w, device in ways:
                 m_copy(0, c, w, device, 0).start()
-        m_y.append([go(mid[c].at[mine], mid[c].at[mine], at("y", yo(t))) for t in range(1, NY)])
+        m_y[c] = [go(mid[c].at[mine], mid[c].at[mine], at("y", yo(t))) for t in range(1, NY)]
+        if c == 1:
+            mid_y[mine] = grad_mid(early)
+            early_gather(0)
 
     def gather_first(c):
-        if c > 0:
+        if c == 0:
             for w, device in ways:
                 m_copy(0, c, w, device, 0).start()
         for t in range(1, NY):
@@ -331,6 +439,7 @@
         for i in range(1, NZ):
             total += gzr[i].astype(F32)
         gb_out[...] = total[8:9]
+        store(gb_store)
         gall[k, x, hy] = total[0:8]
         copies = [go(gall.at[k, x, hy], gall.at[k, x, hy], y8(d)) for d in range(1, NH * NY)]
         yield
@@ -339,9 +448,10 @@
         yield
         received(copies)
         k_copy = go(gall.at[k], gall.at[k], other)
+        store(pltpu.make_async_copy(gall.at[k], gw_hbm.at[k], local.at[10]))
         yield
         k_copy.wait_recv()
-        gw_out[...] = gall[...].reshape(F, F)
+        store(pltpu.make_async_copy(gall.at[1 - k], gw_hbm.at[1 - k], local.at[11]))
         yield
 
     def hp(dh):
@@ -356,27 +466,34 @@
             k_copies.append(go(ks.at[c, j], kr.at[c, j], other))
         yield
 
-        def term(j):
+        def back_term(j):
             dh, dx = turns[j]
             return hist[c, tab[BL + place(xo(dx), hp(dh), k)]] + kr[c, j].astype(F32)
 
-        x_copies = {0: [], 1: []}
-        for j, (dh, dx) in enumerate(turns):
-            k_copies[j].wait_recv()
-            if dx:
-                xs[c, dh, dx - 1] = term(j).astype(BF16)
-                x_copies[dh].append(go(xs.at[c, dh, dx - 1], xr.at[c, dh, dx - 1], at("x", xo(dx))))
-        yield
-        for dh in (1, 0):
-            received(x_copies[dh])
-            total = term(turns.index((dh, 0)))
+        def x_sends(dh):
+            copies = []
+            for j, (dj, dx) in enumerate(turns):
+                if dj == dh:
+                    k_copies[j].wait_recv()
+                    if dx:
+                        xs[c, dh, dx - 1] = back_term(j).astype(BF16)
+                        copies.append(go(xs.at[c, dh, dx - 1], xr.at[c, dh, dx - 1], at("x", xo(dx))))
+            return copies
+
+        def x_sum(dh, copies):
+            received(copies)
+            total = back_term(turns.index((dh, 0)))
             for i in range(NX - 1):
                 total += xr[c, dh, i].astype(F32)
-            if dh:
-                hs[c] = total.astype(BF16)
-                h_copy = go(hs.at[c], hr.at[c], partner)
-            else:
-                own_sum[c] = total
+            return total
+
+        copies = x_sends(1)
+        yield
+        hs[c] = x_sum(1, copies).astype(BF16)
+        h_copy = go(hs.at[c], hr.at[c], partner)
+        copies = x_sends(0)
+        yield
+        own_sum[c] = x_sum(0, copies)
         yield
         h_copy.wait_recv()
         gin_out[:, cols[c]] = (own_sum[c] + hr[c].astype(F32)).astype(BF16)
@@ -384,34 +501,44 @@
 
     grads = gradients()
     backs = [back(c) for c in chunks]
+    gather_first(1)
+    next(grads)
+    early_gather(1)
+    gather_step(1, 1)
+    next(grads)
+    early_gather(2)
+    gather_step(2, 1)
+    early_gather(3)
+    gather_step(3, 1)
+    next(grads)
     gather_first(0)
-    next(grads)
+    early_gather(4)
+    gather_last(1)
     gather_step(1, 0)
-    next(grads)
+    products(1, lambda i: mid[1][i], BR, BP, 0)
+    next(backs[1])
     gather_step(2, 0)
-    gather_first(1)
+    next(backs[1])
+    next(grads)
     gather_step(3, 0)
-    next(grads)
-    gather_step(1, 1)
+    next(backs[1])
+    next(backs[1])
     gather_last(0)
-    products(0, mid, BR, BP, 0)
+    received(e_y)
+    next(grads)
+    products(0, lambda i: jnp.concatenate([mid[0][i], mid_y[i]], axis=1), BR, BP, 0)
     next(backs[0])
-    gather_step(2, 1)
-    next(backs[0])
-    next(grads)
-    gather_step(3, 1)
-    next(backs[0])
-    next(grads)
-    gather_last(1)
-    products(1, mid, BR, BP, 0)
     next(backs[1])
     next(backs[0])
     next(grads)
-    next(backs[1])
-    next(grads)
-    next(backs[1])
-    next(backs[1])
-    next(grads)
+    next(backs[0])
+    next(backs[0])
+    next(grads)
+    next(backs[0])
+    store(gin_store)
+    next(grads)
+    for c in stores:
+        c.wait()
 
     def sent(t, carry):
         for c in chunks:
@@ -422,6 +549,9 @@
         return carry
 
     lax.fori_loop(0, NY, sent, 0)
+    for n in range(4):
+        for w, device in ways:
+            e_copy(n, w, device).wait_send()
     for c in pending:
         c.wait_send()
     assert used[0] <= SEMS
@@ -430,17 +560,19 @@
 CHUNKS = 2
 TURNS = (1, 3, 2)
 W = F // CHUNKS
-SEMS = 256
+V = W // 2
+SEMS = 320
 
 
 def hand_over(*refs):
-    for source, target in zip(refs[: len(refs) // 2], refs[len(refs) // 2 :]):
+    half = len(refs) // 2
+    for source, target in zip(refs[:half], refs[half:]):
         target[...] = source[...]
 
 
 def on_device(features, blocks, positions, counts, weight, bias, cotangent):
     smem = pl.BlockSpec(memory_space=pltpu.SMEM)
-    vmem = pl.BlockSpec(memory_space=pltpu.VMEM)
+    anywhere = pl.BlockSpec(memory_space=pl.ANY)
     table = pl.pallas_call(
         link_slots,
         out_shape=jax.ShapeDtypeStruct((TABLE,), jnp.int32),
@@ -451,38 +583,56 @@
     def chunk(*lead, rows=B, dtype=BF16):
         return pltpu.VMEM((CHUNKS, *lead, rows, W), dtype)
 
-    def part(*lead):
-        return pltpu.VMEM((*lead, B, W), BF16)
+    def part(*lead, rows=B, cols=W, dtype=BF16):
+        return pltpu.VMEM((*lead, rows, cols), dtype)
+
+    def pair(*lead, rows=B, dtype=BF16):
+        return part(*lead, rows=rows, cols=V, dtype=dtype), part(*lead, rows=rows, dtype=dtype)
 
     def full(*lead, rows, dtype=F32):
         return pltpu.VMEM((*lead, rows, F), dtype)
 
     outs = [
         jax.ShapeDtypeStruct((B, F), BF16),
-        jax.ShapeDtypeStruct((F, F), F32),
+        jax.ShapeDtypeStruct((NK, NX, NH * NY, 8, F), F32),
         jax.ShapeDtypeStruct((1, F), F32),
         jax.ShapeDtypeStruct((B, F), BF16),
     ]
     results = pl.pallas_call(
         layer,
         out_shape=outs,
-        in_specs=[smem, vmem, pl.BlockSpec(memory_space=pl.ANY), vmem, vmem, vmem],
-        out_specs=[vmem] * 4,
+        in_specs=[anywhere] * 6,
+        out_specs=[anywhere] * 4,
         scratch_shapes=[
+            pltpu.SMEM((TABLE,), jnp.int32),
+            pltpu.VMEM((F, F), BF16),
+            pltpu.VMEM((1, F), F32),
+            pltpu.VMEM((B, F), BF16),
+            pltpu.VMEM((B, F), BF16),
+            pltpu.VMEM((1, F), F32),
+            pltpu.VMEM((B, F), BF16),
             pltpu.VMEM((SLOTS, B, B), BF16),
             part(TC),
             part(TC),
             chunk(SLOTS + 1, dtype=F32),
-            chunk(2, NY, rows=HALF),
-            chunk(2, NY, rows=HALF),
-            chunk(2, 3, NY),
-            chunk(2, 3, NY),
-            chunk(3),
-            chunk(3),
+            pair(2, NY, rows=HALF),
+            pair(2, NY, rows=HALF),
+            pair(2, 3, NY),
+            pair(2, 3, NY),
+            pair(3),
+            pair(3),
+            pair(dtype=F32),
+            part(3, NZ, cols=V),
+            part(3, NZ, cols=V),
+            part(2, rows=HALF, cols=V),
+            part(2, rows=HALF, cols=V),
+            part(2, 3, cols=V),
+            part(2, 3, cols=V),
             chunk(dtype=F32),
             full(rows=B, dtype=BF16),
+            part(TR, cols=V),
             part(TR),
-            part(TR),
+            part(TR, cols=V),
             chunk(8),
             chunk(8),
             chunk(2, 3),
@@ -500,14 +650,15 @@
             full(NK, NX, NH * NY, rows=8),
             pltpu.SemaphoreType.DMA((SEMS,)),
             pltpu.SemaphoreType.DMA((SEMS,)),
-            pltpu.SemaphoreType.DMA,
+            pltpu.SemaphoreType.DMA((12,)),
         ],
         compiler_params=pltpu.CompilerParams(
             collective_id=0, has_side_effects=True, vmem_limit_bytes=56 * 2**20
         ),
     )(table, features, blocks.reshape(SLOTS, B, B), weight, bias.reshape(1, F), cotangent)
+    vmem = pl.BlockSpec(memory_space=pltpu.VMEM)
     act, gw, gb, gin = pl.pallas_call(hand_over, out_shape=outs, in_specs=[vmem] * 4, out_specs=[vmem] * 4)(*results)
-    return act, gw, gb.reshape(F), gin
+    return act, gw.reshape(F, F), gb.reshape(F), gin
 
 
 def solution(mesh):

time: 157 us -> 149 us (0.949)
  Pallas kernels: 155 us -> 147 us
    pallas_call x1, Pallas kernels: 151 us -> 142 us  [on_device(): pl.pallas_call(layer, out_shape=outs, in_specs=[anywhere] * 6, out_specs=...]
where the time goes in v3:
time: 149 us; the launch traced here: 148 us
  Pallas kernels  147 us (99%)
    pallas_call x1, Pallas kernels, on_device(): pl.pallas_call(layer, out_shape=outs, in_specs=[anywhere] * 6, out_specs=...  142 us

profile of v3, /device:TPU:56, one launch (start us, length us, event | category | flops | bytes accessed | tf_op | source)
XLA Modules:
  0.0 148.0 jit_solution(15414944128950795581)
XLA Ops:
  1.3 2.1 %shard_map.102.tab_hbm = s32[240]{0:T(256)} custom-call(s32[48]{0:T(128)} %bitcast.9, s32[1]{0:T(128)} %bitcast.6.cnt), custom_call_target="tpu_custom_call" | custom-call | tf_op jit(solution)/shard_map/pallas_call | solution.py:576
  3.4 142.2 %shard_map.103 = (bf16[128,512]{1,0:T(8,128)(2,1)}, f32[2,4,8,8,512]{4,3,2,1,0:T(8,128)}, f32[1,512]{1,0:T(1,128)}, bf16[128,512]{1,0:T(8,128)(2,1)}) custom-call(s32[240]{0:T(256)} %shard_map.102.tab_hbm, bf16[128,512]{1,0:T(8,128)(2,1)} %feat_hbm.1, bf16[48,128,128]{2,1,0:T(8,128)(2,1)} %bitcast.7, bf16[512,512]{1,0:T(8,128)(2,1)} %weight_hbm.1, ...), custom_call_target="tpu_custom_call" | custom-call | tf_op jit(solution)/shard_map/pallas_call | solution.py:601
  145.6 2.4 %shard_map.104 = (bf16[128,512]{1,0:T(8,128)(2,1)}, f32[2,4,8,8,512]{4,3,2,1,0:T(8,128)}, f32[1,512]{1,0:T(1,128)}, bf16[128,512]{1,0:T(8,128)(2,1)}) custom-call(bf16[128,512]{1,0:T(8,128)(2,1)} %get-tuple-element.12.refs_0_, f32[2,4,8,8,512]{4,3,2,1,0:T(8,128)} %get-tuple-element.13.refs_1_, f32[1,512]{1,0:T(1,128)} %get-tuple-element.14.refs_2_, ...), custom_call_target="tpu_custom_call" | custom-call | tf_op jit(solution)/shard_map/pallas_call | solution.py:660

commit v4 on v3

--- a/solution.py
+++ b/solution.py
@@ -120,50 +120,61 @@
         c.wait()
     pl.semaphore_wait(barrier, len(greeted))
 
-    used = [0]
-    pending = []
+    used, leaving = [0], []
 
     def ids(count):
         first = used[0]
         used[0] += count
         return first
 
-    def copy(src, dst, device, n):
+    def leaves(ref):
+        leaving.append(ref)
+        return len(leaving) - 1
+
+    def copy(src, dst, device, sent, n):
         return pltpu.make_async_remote_copy(
-            src_ref=src, dst_ref=dst, send_sem=send.at[n], recv_sem=recv.at[n], device_id=device, device_id_type=MESH
+            src_ref=src, dst_ref=dst, send_sem=send.at[sent], recv_sem=recv.at[n], device_id=device, device_id_type=MESH
         )
 
-    def go(src, dst, device):
-        c = copy(src, dst, device, ids(1))
+    def go(src, dst, device, sent, n=None):
+        c = copy(src, dst, device, sent, ids(1) if n is None else n)
         c.start()
-        pending.append(c)
         return c
 
     def received(copies):
         for c in copies:
             c.wait_recv()
 
+    def together(sources, target, devices, ref):
+        sent, n = leaves(ref), ids(1)
+        for source, device in zip(sources, devices):
+            go(source, target, device, sent, n)
+        return copy(ref, ref, other, sent, n)
+
     def features(c):
-        def whole(i, device):
-            return go(fall[c].at[i], fall[c].at[i], device)
+        sent, cross = leaves(fall[c].at[pl.ds(0, 15)]), ids(1)
+
+        def whole(i, device, n=None):
+            return go(fall[c].at[i], fall[c].at[i], device, sent, n)
 
         to_far = whole(own, partner)
         own_x = [whole(own, at("x", xo(d))) for d in TURNS]
-        crossed = [whole(own, other)]
+        whole(own, other, cross)
         yield
         to_far.wait_recv()
         far_x = [whole(far, at("x", xo(d))) for d in TURNS]
-        crossed.append(whole(far, other))
+        whole(far, other, cross)
         yield
         for d, c_x in zip(TURNS, own_x):
             c_x.wait_recv()
-            crossed.append(whole(place(xo(NX - d), h, k), other))
+            whole(place(xo(NX - d), h, k), other, cross)
         yield
         for d, c_x in zip(TURNS, far_x):
             c_x.wait_recv()
-            crossed.append(whole(place(xo(NX - d), 1 - h, k), other))
-        yield
-        received(crossed)
+            whole(place(xo(NX - d), 1 - h, k), other, cross)
+        yield
+        eight = fall[c].at[pl.ds(0, TC // NK)]
+        copy(eight, eight, other, sent, cross).wait_recv()
         yield
 
     step = 8
@@ -189,12 +200,13 @@
         lax.fori_loop(0, SLOTS // step, one, 0)
 
     z_ids = ids(32 * CHUNKS)
+    z_sent = [(leaves(zs1[c]), leaves(zs[c])) for c in chunks]
 
     def z_copy(n, c, w, device, t):
         sem = z_ids + ((c * 4 + n) * 2 + w) * NY + t
         if n == 0:
-            return copy(zs1[c].at[w, t], zr1[c].at[w, t], device, sem)
-        return copy(zs[c].at[w, n - 1, t], zr[c].at[w, n - 1, t], device, sem)
+            return copy(zs1[c].at[w, t], zr1[c].at[w, t], device, z_sent[c][0], sem)
+        return copy(zs[c].at[w, n - 1, t], zr[c].at[w, n - 1, t], device, z_sent[c][1], sem)
 
     def term(c, row, rows=slice(0, B)):
         return hist[c, tab[FL + row], rows, z_hist[c]]
@@ -223,13 +235,14 @@
     y_copies = []
 
     def scatter_y(c):
+        sent = leaves(ys[c])
         for t in range(NY):
             for w, device in ways:
                 z_copy(3, c, w, device, t).wait_recv()
             total = term(c, yo(1 + t) * NZ + z) + zr[c][0, 2, t].astype(F32) + zr[c][1, 2, t].astype(F32)
             if t < NY - 1:
                 ys[c][t] = total.astype(BF16)
-                y_copies.append(go(ys[c].at[t], yr[c].at[t], at("y", yo(1 + t))))
+                y_copies.append(go(ys[c].at[t], yr[c].at[t], at("y", yo(1 + t)), sent))
             else:
                 oz[c][...] = total
 
@@ -237,6 +250,7 @@
     groups = (slice(0, 1), slice(1, 3), slice(3, 5), slice(5, 7), slice(7, 8))
     early_hist = slice(V, 2 * V)
     early_y, early_z = [], {}
+    early_sent = [leaves(ref) for ref in (y1s, y2s1, y2s)]
 
     def early_send():
         for group in groups:
@@ -245,7 +259,7 @@
                 for p in range(group.start, group.stop):
                     y1s[d - 1, p] = hist[0, tab[FL + yo(d) * NZ + zo(order[p])], :, early_hist].astype(BF16)
                 part = pl.ds(group.start, group.stop - group.start)
-                copies.append(go(y1s.at[d - 1, part], y1r.at[d - 1, part], at("y", yo(d))))
+                copies.append(go(y1s.at[d - 1, part], y1r.at[d - 1, part], at("y", yo(d)), early_sent[0]))
             early_y.append(copies)
 
     def early_term(p, rows=slice(0, B)):
@@ -259,7 +273,7 @@
         for w, device in ways:
             if n == 0:
                 y2s1[w] = early_term(0, halves[w]).astype(BF16)
-                early_z[0, w] = go(y2s1.at[w], y2r1.at[w], device)
+                early_z[0, w] = go(y2s1.at[w], y2r1.at[w], device, early_sent[1])
                 continue
             early_z[n - 1, w].wait_recv()
             p = 2 * n - 1 + w
@@ -268,7 +282,7 @@
                 y2s[w, 0, halves[1 - w]] = early_term(p, halves[1 - w]).astype(BF16)
             else:
                 y2s[w, n - 1] = (early_term(p) + y2r[w, n - 2].astype(F32)).astype(BF16)
-            early_z[n, w] = go(y2s.at[w, n - 1], y2r.at[w, n - 1], device)
+            early_z[n, w] = go(y2s.at[w, n - 1], y2r.at[w, n - 1], device, early_sent[2])
 
     def early_last():
         received(early_y[4])
@@ -281,6 +295,7 @@
     next(later)
     next(first)
     next(first)
+    next(later)
     next(first)
     for c in early_in:
         c.wait()
@@ -289,7 +304,6 @@
     early_send()
     next(later)
     scatter_step(1, 0)
-    next(later)
     next(later)
     early_step(0)
     scatter_step(2, 0)
@@ -321,6 +335,7 @@
     grad_pre = (cot[...].astype(F32) * sigma * (1.0 + pre * (1.0 - sigma))).astype(BF16)
     mine = y * NZ + z
     m_ids = ids(32 * CHUNKS)
+    m_sent = [leaves(mid[c].at[pl.ds(0, 31)]) for c in chunks]
 
     def m_copy(n, c, w, device, t):
         row = yo(NY - t) * NZ + zo(NZ - n if w == 0 else n)
@@ -328,7 +343,7 @@
         ref = mid[c].at[row]
         if n == 3:
             ref = mid[c].at[row, pl.ds(w * HALF, HALF)]
-        return copy(ref, ref, device, sem)
+        return copy(ref, ref, device, m_sent[c], sem)
 
     def grad_mid(part):
         return lax.dot_general(
@@ -336,19 +351,19 @@
         ).astype(BF16)
 
     m_y = {}
-    e_ids = ids(8)
-    e_y = []
+    e_ids, e_y = ids(8), ids(1)
+    e_sent = leaves(mid_y.at[pl.ds(0, 31)])
 
     def e_copy(n, w, device):
         row = y * NZ + zo(NZ - n if w == 0 else n)
         ref = mid_y.at[row]
         if n == 3:
             ref = mid_y.at[row, pl.ds(w * HALF, HALF)]
-        return copy(ref, ref, device, e_ids + n * 2 + w)
+        return copy(ref, ref, device, e_sent, e_ids + n * 2 + w)
 
     def e_spread(row):
         for t in range(1, NY):
-            e_y.append(go(mid_y.at[row], mid_y.at[row], at("y", yo(t))))
+            go(mid_y.at[row], mid_y.at[row], at("y", yo(t)), e_sent, e_y)
 
     def early_gather(n):
         for w, device in ways:
@@ -369,7 +384,7 @@
         if c == 1:
             for w, device in ways:
                 m_copy(0, c, w, device, 0).start()
-        m_y[c] = [go(mid[c].at[mine], mid[c].at[mine], at("y", yo(t))) for t in range(1, NY)]
+        m_y[c] = [go(mid[c].at[mine], mid[c].at[mine], at("y", yo(t)), m_sent[c]) for t in range(1, NY)]
         if c == 1:
             mid_y[mine] = grad_mid(early)
             early_gather(0)
@@ -408,46 +423,51 @@
                 agg[:, kk * 256 : (kk + 1) * 256], grad_pre, (((0,), (0,)), ((), ())), preferred_element_type=F32
             )
             g0[kk, 256:264] = bias_rows
-        k_copy = go(g0.at[1 - k], gk, other)
+        k_copy = go(g0.at[1 - k], gk, other, leaves(gk))
         yield
         k_copy.wait_recv()
         for i in range(NX):
             gx[i, 0:64] = g0[k, i * 64 : (i + 1) * 64] + gk[i * 64 : (i + 1) * 64]
             gx[i, 64:72] = g0[k, 256:264] + gk[256:264]
         gxr[x] = gx[x]
-        copies = [go(gx.at[xo(d)], gxr.at[x], at("x", xo(d))) for d in range(1, NX)]
-        yield
-        received(copies)
+        x_devices = [at("x", xo(d)) for d in range(1, NX)]
+        y_devices = [y8(d) for d in range(1, NH * NY)]
+        copies = together([gx.at[xo(d)] for d in range(1, NX)], gxr.at[x], x_devices, gxr.at[pl.ds(0, 3)])
+        yield
+        copies.wait_recv()
         bias_sum = gxr[0, 64:72] + gxr[1, 64:72] + gxr[2, 64:72] + gxr[3, 64:72]
         for i in range(NH * NY):
             rows = slice(i * 8, (i + 1) * 8)
             gy[i, 0:8] = gxr[0, rows] + gxr[1, rows] + gxr[2, rows] + gxr[3, rows]
             gy[i, 8:16] = bias_sum
         gyr[hy] = gy[hy]
-        copies = [go(gy.at[lax.rem(hy + d, NH * NY)], gyr.at[hy], y8(d)) for d in range(1, NH * NY)]
-        yield
-        received(copies)
+        sources = [gy.at[lax.rem(hy + d, NH * NY)] for d in range(1, NH * NY)]
+        copies = together(sources, gyr.at[hy], y_devices, gyr.at[pl.ds(0, 7)])
+        yield
+        copies.wait_recv()
         total = gyr[0]
         for i in range(1, NH * NY):
             total += gyr[i]
         gz[...] = total.astype(BF16)
         gzr[z] = gz[...]
-        copies = [go(gz, gzr.at[z], at("z", zo(d))) for d in range(1, NZ)]
-        yield
-        received(copies)
+        copies = together([gz] * 7, gzr.at[z], [at("z", zo(d)) for d in range(1, NZ)], gzr.at[pl.ds(0, 7)])
+        yield
+        copies.wait_recv()
         total = gzr[0].astype(F32)
         for i in range(1, NZ):
             total += gzr[i].astype(F32)
         gb_out[...] = total[8:9]
         store(gb_store)
         gall[k, x, hy] = total[0:8]
-        copies = [go(gall.at[k, x, hy], gall.at[k, x, hy], y8(d)) for d in range(1, NH * NY)]
-        yield
-        received(copies)
-        copies = [go(gall.at[k, x], gall.at[k, x], at("x", xo(d))) for d in range(1, NX)]
-        yield
-        received(copies)
-        k_copy = go(gall.at[k], gall.at[k], other)
+        piece = gall.at[k, x, hy]
+        copies = together([piece] * 7, piece, y_devices, gall.at[0, 0, pl.ds(0, 7)])
+        yield
+        copies.wait_recv()
+        piece = gall.at[k, x]
+        copies = together([piece] * 3, piece, x_devices, gall.at[0, pl.ds(0, 3)])
+        yield
+        copies.wait_recv()
+        k_copy = go(gall.at[k], gall.at[k], other, leaves(gall.at[0]))
         store(pltpu.make_async_copy(gall.at[k], gw_hbm.at[k], local.at[10]))
         yield
         k_copy.wait_recv()
@@ -460,10 +480,11 @@
     turns = [(dh, dx) for dh in (1, 0) for dx in (*TURNS, 0)]
 
     def back(c):
+        sent_k, sent_x = leaves(ks.at[c]), leaves(xs.at[c])
         k_copies = []
         for j, (dh, dx) in enumerate(turns):
             ks[c, j] = hist[c, tab[BL + place(xo(dx), hp(dh), 1 - k)]].astype(BF16)
-            k_copies.append(go(ks.at[c, j], kr.at[c, j], other))
+            k_copies.append(go(ks.at[c, j], kr.at[c, j], other, sent_k))
         yield
 
         def back_term(j):
@@ -477,7 +498,7 @@
                     k_copies[j].wait_recv()
                     if dx:
                         xs[c, dh, dx - 1] = back_term(j).astype(BF16)
-                        copies.append(go(xs.at[c, dh, dx - 1], xr.at[c, dh, dx - 1], at("x", xo(dx))))
+                        copies.append(go(xs.at[c, dh, dx - 1], xr.at[c, dh, dx - 1], at("x", xo(dx)), sent_x))
             return copies
 
         def x_sum(dh, copies):
@@ -490,7 +511,7 @@
         copies = x_sends(1)
         yield
         hs[c] = x_sum(1, copies).astype(BF16)
-        h_copy = go(hs.at[c], hr.at[c], partner)
+        h_copy = go(hs.at[c], hr.at[c], partner, leaves(hs.at[c]))
         copies = x_sends(0)
         yield
         own_sum[c] = x_sum(0, copies)
@@ -524,7 +545,8 @@
     next(backs[1])
     next(backs[1])
     gather_last(0)
-    received(e_y)
+    most = mid_y.at[pl.ds(0, NZ * (NY - 1))]
+    copy(most, most, up, e_sent, e_y).wait_recv()
     next(grads)
     products(0, lambda i: jnp.concatenate([mid[0][i], mid_y[i]], axis=1), BR, BP, 0)
     next(backs[0])
@@ -540,28 +562,16 @@
     for c in stores:
         c.wait()
 
-    def sent(t, carry):
-        for c in chunks:
-            for n in range(4):
-                for w, device in ways:
-                    z_copy(n, c, w, device, t).wait_send()
-                    m_copy(n, c, w, device, t).wait_send()
-        return carry
-
-    lax.fori_loop(0, NY, sent, 0)
-    for n in range(4):
-        for w, device in ways:
-            e_copy(n, w, device).wait_send()
-    for c in pending:
-        c.wait_send()
-    assert used[0] <= SEMS
+    for n, ref in enumerate(leaving):
+        copy(ref, ref, other, n, 0).wait_send()
+    assert used[0] == ARRIVE and len(leaving) == LEAVE
 
 
 CHUNKS = 2
 TURNS = (1, 3, 2)
 W = F // CHUNKS
 V = W // 2
-SEMS = 320
+LEAVE, ARRIVE = 27, 225
 
 
 def hand_over(*refs):
@@ -648,8 +658,8 @@
             full(rows=16, dtype=BF16),
             full(NZ, rows=16, dtype=BF16),
             full(NK, NX, NH * NY, rows=8),
-            pltpu.SemaphoreType.DMA((SEMS,)),
-            pltpu.SemaphoreType.DMA((SEMS,)),
+            pltpu.SemaphoreType.DMA((LEAVE,)),
+            pltpu.SemaphoreType.DMA((ARRIVE,)),
             pltpu.SemaphoreType.DMA((12,)),
         ],
         compiler_params=pltpu.CompilerParams(

time: 149 us -> 146 us (0.980)
  Pallas kernels: 147 us -> 144 us
    pallas_call x1, Pallas kernels: 142 us -> 139 us  [on_device(): pl.pallas_call(layer, out_shape=outs, in_specs=[anywhere] * 6, out_specs=...]
where the time goes in v4:
time: 146 us; the launch traced here: 145 us
  Pallas kernels  144 us (99%)
    pallas_call x1, Pallas kernels, on_device(): pl.pallas_call(layer, out_shape=outs, in_specs=[anywhere] * 6, out_specs=...  139 us

profile of v4, /device:TPU:56, one launch (start us, length us, event | category | flops | bytes accessed | tf_op | source)
XLA Modules:
  0.0 145.1 jit_solution(17731863647453077504)
XLA Ops:
  1.3 2.1 %shard_map.102.tab_hbm = s32[240]{0:T(256)} custom-call(s32[48]{0:T(128)} %bitcast.9, s32[1]{0:T(128)} %bitcast.6.cnt), custom_call_target="tpu_custom_call" | custom-call | tf_op jit(solution)/shard_map/pallas_call | solution.py:586
  3.4 139.4 %shard_map.103 = (bf16[128,512]{1,0:T(8,128)(2,1)}, f32[2,4,8,8,512]{4,3,2,1,0:T(8,128)}, f32[1,512]{1,0:T(1,128)}, bf16[128,512]{1,0:T(8,128)(2,1)}) custom-call(s32[240]{0:T(256)} %shard_map.102.tab_hbm, bf16[128,512]{1,0:T(8,128)(2,1)} %feat_hbm.1, bf16[48,128,128]{2,1,0:T(8,128)(2,1)} %bitcast.7, bf16[512,512]{1,0:T(8,128)(2,1)} %weight_hbm.1, ...), custom_call_target="tpu_custom_call" | custom-call | tf_op jit(solution)/shard_map/pallas_call | solution.py:611
  142.8 2.4 %shard_map.104 = (bf16[128,512]{1,0:T(8,128)(2,1)}, f32[2,4,8,8,512]{4,3,2,1,0:T(8,128)}, f32[1,512]{1,0:T(1,128)}, bf16[128,512]{1,0:T(8,128)(2,1)}) custom-call(bf16[128,512]{1,0:T(8,128)(2,1)} %get-tuple-element.12.refs_0_, f32[2,4,8,8,512]{4,3,2,1,0:T(8,128)} %get-tuple-element.13.refs_1_, f32[1,512]{1,0:T(1,128)} %get-tuple-element.14.refs_2_, ...), custom_call_target="tpu_custom_call" | custom-call | tf_op jit(solution)/shard_map/pallas_call | solution.py:670

commit v5 on v4

--- a/solution.py
+++ b/solution.py
@@ -44,7 +44,7 @@
         tab[BL + c] = jnp.where(live, s, last_c)
         return carry
 
-    lax.fori_loop(0, SLOTS, one, 0)
+    lax.fori_loop(0, SLOTS, one, 0, unroll=4)
 
 
 def layer(
@@ -305,21 +305,21 @@
     next(later)
     scatter_step(1, 0)
     next(later)
-    early_step(0)
     scatter_step(2, 0)
     next(later)
     products(1, lambda i: fall[1][i], FC, FP, 1)
     scatter_step(0, 1)
+    early_step(0)
     scatter_step(3, 0)
+    scatter_step(1, 1)
     early_step(1)
-    scatter_step(1, 1)
-    early_step(2)
     scatter_y(0)
     scatter_step(2, 1)
+    early_step(2)
+    scatter_step(3, 1)
     early_step(3)
-    scatter_step(3, 1)
+    scatter_y(1)
     early_last()
-    scatter_y(1)
     received(y_copies)
     for c in chunks:
         agg[:, z_cols[c]] = (

time: 146 us -> 145 us (level)
  no operation moved by 1% of the time
where the time goes in v5:
time: 145 us; the launch traced here: 144 us
  Pallas kernels  143 us (99%)
    pallas_call x1, Pallas kernels, on_device(): pl.pallas_call(layer, out_shape=outs, in_specs=[anywhere] * 6, out_specs=...  139 us

profile of v5, /device:TPU:56, one launch (start us, length us, event | category | flops | bytes accessed | tf_op | source)
XLA Modules:
  0.0 144.3 jit_solution(15889426436978637075)
XLA Ops:
  1.3 1.7 %shard_map.102.tab_hbm = s32[240]{0:T(256)} custom-call(s32[48]{0:T(128)} %bitcast.9, s32[1]{0:T(128)} %bitcast.6.cnt), custom_call_target="tpu_custom_call" | custom-call | tf_op jit(solution)/shard_map/pallas_call | solution.py:586
  3.0 138.9 %shard_map.103 = (bf16[128,512]{1,0:T(8,128)(2,1)}, f32[2,4,8,8,512]{4,3,2,1,0:T(8,128)}, f32[1,512]{1,0:T(1,128)}, bf16[128,512]{1,0:T(8,128)(2,1)}) custom-call(s32[240]{0:T(256)} %shard_map.102.tab_hbm, bf16[128,512]{1,0:T(8,128)(2,1)} %feat_hbm.1, bf16[48,128,128]{2,1,0:T(8,128)(2,1)} %bitcast.7, bf16[512,512]{1,0:T(8,128)(2,1)} %weight_hbm.1, ...), custom_call_target="tpu_custom_call" | custom-call | tf_op jit(solution)/shard_map/pallas_call | solution.py:611
  141.9 2.4 %shard_map.104 = (bf16[128,512]{1,0:T(8,128)(2,1)}, f32[2,4,8,8,512]{4,3,2,1,0:T(8,128)}, f32[1,512]{1,0:T(1,128)}, bf16[128,512]{1,0:T(8,128)(2,1)}) custom-call(bf16[128,512]{1,0:T(8,128)(2,1)} %get-tuple-element.12.refs_0_, f32[2,4,8,8,512]{4,3,2,1,0:T(8,128)} %get-tuple-element.13.refs_1_, f32[1,512]{1,0:T(1,128)} %get-tuple-element.14.refs_2_, ...), custom_call_target="tpu_custom_call" | custom-call | tf_op jit(solution)/shard_map/pallas_call | solution.py:670
